TPU v7x, 32 devices: a whole 2x2x4 slice. The times are simulated.
32 devices in a mesh: dp: 16 (over z, y, core), tensor: 2 (over x).
Axes of the slice: x: 2, y: 2, z: 4, core: 2. Of those that a mesh axis runs over, the one named last changes fastest.
Arguments:
- tokens: bfloat16 [1, 16384, 1024], P(None, 'dp', 'tensor'), may hold values from -6 to 6
- cotangent: bfloat16 [1, 16384, 1024], P(None, 'dp', 'tensor'), may hold values from -6 to 6
- segments: int32 [1, 16384], P(None, 'dp'), may hold values from 0 to 7, as said below
- owners: int32 [6], replicated, may hold values from 0 to 3, as said below
- attn_master: float32 [2, 4096, 1024], P(None, 'dp', 'tensor')
- attn_first: float32 [2, 4096, 1024], P(None, 'dp', 'tensor')
- attn_second: float32 [2, 4096, 1024], P(None, 'dp', 'tensor'), as said below
- mlp_master: float32 [1, 4096, 4096], P(None, 'dp', 'tensor')
- mlp_first: float32 [1, 4096, 4096], P(None, 'dp', 'tensor')
- mlp_second: float32 [1, 4096, 4096], P(None, 'dp', 'tensor'), as said below
- ssm_params: float32 [3, 1024, 16], P(None, 'tensor'), as said below
- ssm_first: float32 [3, 1024, 16], P(None, 'tensor')
- ssm_second: float32 [3, 1024, 16], P(None, 'tensor'), as said below
- norm_gains: float32 [2, 1024], P(None, 'tensor'), may hold values from 0.5 to 1.5
- gains_first: float32 [2, 1024], P(None, 'tensor')
- gains_second: float32 [2, 1024], P(None, 'tensor'), as said below
Outputs:
- block_out: bfloat16 [1, 16384, 1024], P(None, 'dp', 'tensor')
- grad_tokens: float32 [1, 16384, 1024], P(None, 'dp', 'tensor')
- attn_grad: float32 [2, 4096, 1024], P(None, 'dp', 'tensor')
- attn_first_new: float32 [2, 4096, 1024], P(None, 'dp', 'tensor')
- attn_second_new: float32 [2, 4096, 1024], P(None, 'dp', 'tensor')
- attn_new: float32 [2, 4096, 1024], P(None, 'dp', 'tensor')
- attn_new_low: bfloat16 [2, 4096, 1024], P(None, 'dp', 'tensor')
- mlp_grad: float32 [1, 4096, 4096], P(None, 'dp', 'tensor')
- mlp_first_new: float32 [1, 4096, 4096], P(None, 'dp', 'tensor')
- mlp_second_new: float32 [1, 4096, 4096], P(None, 'dp', 'tensor')
- mlp_new: float32 [1, 4096, 4096], P(None, 'dp', 'tensor')
- mlp_new_low: bfloat16 [1, 4096, 4096], P(None, 'dp', 'tensor')
- ssm_grad: float32 [3, 1024, 16], P(None, 'tensor')
- ssm_first_new: float32 [3, 1024, 16], P(None, 'tensor')
- ssm_second_new: float32 [3, 1024, 16], P(None, 'tensor')
- ssm_new: float32 [3, 1024, 16], P(None, 'tensor')
- gains_grad: float32 [2, 1024], P(None, 'tensor')
- gains_first_new: float32 [2, 1024], P(None, 'tensor')
- gains_second_new: float32 [2, 1024], P(None, 'tensor')
- gains_new: float32 [2, 1024], P(None, 'tensor')
Inputs may be any that keep to these rules, and one draw needn't show every extreme that they name: `segments`: in each row ids start at 0, never fall, and each row holds exactly 8 documents. No group owns more than 2 of the first four matrices, and one group owns exactly that many; no group owns more than 1 of the last two, so these two have different owners. `attn_second`: positive. `mlp_second`: positive. `ssm_params`: the first row lies between -log(512) / 2 and log(512) / 2. `ssm_second`: positive. `gains_second`: positive.
All inputs are finite; a program needn't handle non-finite values.
Results may differ from a plain program's by a relative error of at most 0.012.
Values may be sent and summed in bfloat16 or wider, within the bound.
No kernel may reach another device: no remote copies, remote signals or barrier semaphores. Data moves between devices by JAX's collectives and lax.ppermute only.
A program may use at most 448 MiB of HBM per device.

v0:
```python
import functools
import itertools

import jax
import jax.numpy as jnp
from jax import lax
from jax.experimental import pallas as pl
from jax.experimental.pallas import tpu as pltpu
from jax.sharding import PartitionSpec as P

D = 1024
HEAD_DIM = 128
FF = 4096
STATE = 16
CTX = 128
BL = 512
OWNER_GROUPS = 4
STEP = 5

epsilon_norm = 1e-05
beta_first = 0.9
beta_second = 0.95
epsilon_adam = 1e-08
matrix_decay = 0.1
masked_score = -1e30
score_scale = HEAD_DIM ** (-0.5)
f32 = jnp.float32
bf16 = jnp.bfloat16
i32 = jnp.int32
SWAP = [(0, 1), (1, 0)]
COST = 1000
TILE = 256
QT = 256
FT = 512
LOG2E = 1.4426950408889634


def dot_nn(left, right):
    return lax.dot_general(left, right, (((1,), (0,)), ((), ())), preferred_element_type=f32)


def dot_nt(left, right):
    return lax.dot_general(left, right, (((1,), (1,)), ((), ())), preferred_element_type=f32)


def dot_tn(left, right):
    return lax.dot_general(left, right, (((0,), (0,)), ((), ())), preferred_element_type=f32)


def call(
    kernel, grid, in_specs, out_specs, out_shape, scratch=(), prefetch=0, flops=0, nbytes=0, room=36
):
    return pl.pallas_call(
        kernel,
        grid_spec=pltpu.PrefetchScalarGridSpec(
            num_scalar_prefetch=prefetch,
            grid=grid,
            in_specs=in_specs,
            out_specs=out_specs,
            scratch_shapes=scratch,
        ),
        out_shape=out_shape,
        name=kernel.__name__,
        compiler_params=pltpu.CompilerParams(vmem_limit_bytes=room * 1024 * 1024),
        cost_estimate=pl.CostEstimate(flops=flops // COST, bytes_accessed=nbytes // COST, transcendentals=0),
    )


def whole(shape):
    return pl.BlockSpec(shape, lambda *_: (0,) * len(shape), pipeline_mode=pl.Buffered(1))


def sds(shape, dtype):
    return jax.ShapeDtypeStruct(shape, dtype)


def hbm(*values):
    held = tuple(pltpu.with_memory_space_constraint(v, pltpu.HBM) for v in values)
    return held[0] if len(held) == 1 else held


def swap_x(values):
    return lax.ppermute(values, "tensor", SWAP)


def gate(value, *others):
    if not others:
        return value
    return lax.optimization_barrier((value,) + others)[0]


def together(*values):
    return lax.optimization_barrier(values)


def gather_rounds():
    return max(lax.axis_size("dp") - 1, 0).bit_length()


def gather_round(held, k):
    step = 1 << k
    count = lax.axis_size("dp")
    other = lax.ppermute(held, "dp", [(i, i ^ step) for i in range(count)])
    later = (lax.axis_index("dp") // step) % 2 == 1
    return jnp.where(
        later,
        jnp.concatenate([other, held], axis=0),
        jnp.concatenate([held, other], axis=0),
    )


def total_dp(values, beside):
    count = lax.axis_size("dp")
    for k in range(gather_rounds()):
        if k == 1:
            values, beside = together(values, beside)
        values = values + lax.ppermute(values, "dp", [(i, i ^ (1 << k)) for i in range(count)])
    return values, beside


def routes(full_count, empty_count):
    groups = range(OWNER_GROUPS)
    ways = []
    for full in itertools.combinations(groups, full_count):
        rest = [g for g in groups if g not in full]
        for empty in itertools.combinations(rest, empty_count):
            ways.append((full, empty))
    return ways


ATTN_WAYS = routes(1, 1) + routes(2, 2)


def way_code(full, empty):
    code = 0
    for g in range(OWNER_GROUPS):
        digit = 2 if g in full else (0 if g in empty else 1)
        code += digit * 3**g
    return code


def one_if(condition):
    return jnp.where(condition, jnp.int32(1), jnp.int32(0))


HOST_MLP, SIDE, WAY, NEAR, ATTN_HERE, MLP_HERE, PLAN_SIZE = 4, 8, 9, 10, 11, 12, 16
ATTN_RATES = [0.5 * D ** (-0.5)] * 3 + [0.5 * (D // 16) ** (-0.5)]
MLP_RATES = [0.5 * D ** (-0.5), 0.5 * FF ** (-0.5)]
IDLE_RATE = 0.5 * D ** (-0.5)


def plan_kernel(owner_ref, here_ref, out_ref, rate_ref):
    groups = range(OWNER_GROUPS)
    side, group = here_ref[0], here_ref[1]
    owner = [owner_ref[m] for m in range(6)]
    slot = [
        sum([one_if(owner[k] == owner[m]) for k in range(m)], jnp.int32(0)) for m in range(4)
    ]
    count = [sum([one_if(owner[m] == g) for m in range(4)], jnp.int32(0)) for g in groups]
    full_rank = [sum([one_if(count[h] == 2) for h in range(g)], jnp.int32(0)) for g in groups]
    empty_rank = [sum([one_if(count[h] == 0) for h in range(g)], jnp.int32(0)) for g in groups]
    taker = [
        sum(
            [
                jnp.where(
                    jnp.logical_and(count[h] == 0, empty_rank[h] == full_rank[g]), jnp.int32(h), 0
                )
                for h in groups
            ],
            jnp.int32(0),
        )
        for g in groups
    ]
    for m in range(4):
        second = sum([jnp.where(owner[m] == g, taker[g], 0) for g in groups], jnp.int32(0))
        out_ref[m] = jnp.where(slot[m] == 0, owner[m], second)
    code = sum([count[g] * 3**g for g in groups], jnp.int32(0))
    out_ref[WAY] = sum(
        [
            jnp.where(code == way_code(*way), jnp.int32(k), 0)
            for k, way in enumerate(ATTN_WAYS)
        ],
        jnp.int32(0),
    )
    low = sum([one_if(owner[m] < 2) for m in (4, 5)], jnp.int32(0))
    near = low == 1
    for k, m in enumerate((4, 5)):
        out_ref[HOST_MLP + 2 * k] = owner[m]
        bit = jnp.where(near, jnp.int32(1), jnp.int32(2))
        out_ref[HOST_MLP + 2 * k + 1] = jnp.bitwise_xor(owner[m], bit)
    out_ref[SIDE] = side
    out_ref[NEAR] = one_if(near)
    out_ref[ATTN_HERE] = sum([one_if(owner[m] == group) for m in range(4)], jnp.int32(0))
    out_ref[MLP_HERE] = sum([one_if(owner[m] == group) for m in (4, 5)], jnp.int32(0))
    for k in range(MLP_HERE + 1, PLAN_SIZE):
        out_ref[k] = jnp.int32(0)
    for place in range(2):
        rate = f32(IDLE_RATE)
        for m in range(4):
            hit = jnp.logical_and(owner[m] == group, slot[m] == place)
            rate = jnp.where(hit, f32(ATTN_RATES[m]), rate)
        rate_ref[place] = rate
    rate = f32(IDLE_RATE)
    for k, m in enumerate((4, 5)):
        rate = jnp.where(owner[m] == group, f32(MLP_RATES[k]), rate)
    rate_ref[2] = rate
    rate_ref[3] = f32(0.0)


def move(values, index, ways, back):
    size = lax.axis_size("dp") // OWNER_GROUPS

    def branch(way):
        pairs = []
        for a, b in zip(*way):
            if back:
                a, b = b, a
            pairs += [(a * size + j, b * size + j) for j in range(size)]
        return lambda v: lax.ppermute(v, "dp", pairs)

    return lax.switch(index, [branch(way) for way in ways], values)


def exchange_groups(values, near):
    size = lax.axis_size("dp") // OWNER_GROUPS

    def across(bit):
        return lax.ppermute(
            values,
            "dp",
            [(g * size + j, (g ^ bit) * size + j) for g in range(OWNER_GROUPS) for j in range(size)],
        )

    return jnp.where(near, across(1), across(2))


def ring_order(count):
    chips = count // 2
    if chips == 8:
        return [0, 2, 4, 6, 7, 5, 3, 1]
    return list(range(chips))


def join_kernel(host_ref, own_ref, other_ref, out_ref):
    @pl.when(pl.program_id(0) == 0)
    def _():
        out_ref[...] = own_ref[...]

    @pl.when(pl.program_id(0) == 1)
    def _():
        out_ref[...] = other_ref[...]


def join_scaled_kernel(
    host_ref, own_ref, other_ref, inverse_ref, gain_ref, gain_other_ref, out_ref
):
    @pl.when(pl.program_id(0) == 0)
    def _():
        out_ref[...] = (own_ref[...].astype(f32) * inverse_ref[...] * gain_ref[...]).astype(bf16)

    @pl.when(pl.program_id(0) == 1)
    def _():
        out_ref[...] = (
            other_ref[...].astype(f32) * inverse_ref[...] * gain_other_ref[...]
        ).astype(bf16)


def join_sides(hosts, own, other, scales=()):
    rows, width = own.shape
    return call(
        join_scaled_kernel if scales else join_kernel,
        (2,),
        [whole(v.shape) for v in (own, other) + tuple(scales)],
        [
            pl.BlockSpec(
                (rows, width), lambda d, s: (0, jnp.where(d == 0, s[SIDE], 1 - s[SIDE]))
            )
        ],
        [pltpu.HBM((rows, 2 * width), bf16)],
        prefetch=1,
        nbytes=8 * rows * width,
        room=12,
    )(hosts, own, other, *scales)[0]


class Ring:
    def __init__(self):
        self.count = lax.axis_size("dp")
        self.chips = self.count // 2
        order = ring_order(self.count)
        here = lax.axis_index("dp")
        self.core = here % 2
        chip = here // 2
        self.place = jnp.where(chip % 2 == 0, chip // 2, 7 - chip // 2) if self.chips == 8 else chip
        self.up = [
            (2 * order[p] + c, 2 * order[(p + 1) % self.chips] + c)
            for p in range(self.chips)
            for c in range(2)
        ]
        self.down = [(b, a) for a, b in self.up]
        self.cores = [(i, i ^ 1) for i in range(self.count)]
        self.far_up = self.chips // 2
        self.far_down = self.chips - 1 - self.far_up

    def chip(self, offset):
        place = (self.place + self.chips + offset) % self.chips
        if self.chips != 8:
            return place
        return jnp.where(place < 4, 2 * place, 15 - 2 * place)

    def start(self, blocks):
        pairs = blocks.reshape((self.chips, 2) + blocks.shape[1:])
        mine = lax.dynamic_index_in_dim(pairs, self.core, 1, keepdims=False)
        theirs = lax.dynamic_index_in_dim(pairs, 1 - self.core, 1, keepdims=False)
        received = lax.ppermute(theirs, "dp", self.cores)

        def part(offset):
            chip = self.chip(offset)
            return lax.dynamic_index_in_dim(mine, chip, 0, keepdims=False).astype(
                f32
            ) + lax.dynamic_index_in_dim(received, chip, 0, keepdims=False).astype(f32)

        return part, part(self.far_up).astype(bf16), part(-self.far_down).astype(bf16)

    def step(self, k, part, up, down):
        if k < self.far_up:
            up = lax.ppermute(up, "dp", self.up)
            if k < self.far_up - 1:
                up = (up.astype(f32) + part(self.far_up - 1 - k)).astype(bf16)
        if k < self.far_down:
            down = lax.ppermute(down, "dp", self.down)
            if k < self.far_down - 1:
                down = (down.astype(f32) + part(k + 1 - self.far_down)).astype(bf16)
        return up, down


def shift_tails(values, by, cross):
    count = lax.axis_size("dp")
    pairs = [
        (2 * i + s, 2 * (i + by) + (1 - s if cross else s))
        for i in range(count)
        for s in range(2)
        if 0 <= i + by < count
    ]
    return lax.ppermute(values, ("dp", "tensor"), pairs)


def first_half():
    return lax.broadcasted_iota(i32, (8, 128), 0) < 4


def flag(condition):
    return jnp.where(condition, f32(1.0), f32(0.0))


def keep_at(seg_ref, t, half):
    return jnp.where(
        half, flag(seg_ref[t + 1] == seg_ref[t]), flag(seg_ref[BL + t + 1] == seg_ref[BL + t])
    )


def chunked(seg_ref, begin, end, plain, kept, carried, back=False):
    size = 8
    count = (end - begin) // size

    def chunk(c, carried):
        first = begin + (count - 1 - c if back else c) * size
        same = jnp.logical_and(
            seg_ref[first] == seg_ref[first + size],
            seg_ref[BL + first] == seg_ref[BL + first + size],
        )

        def run(step):
            def go(carried):
                for k in range(size):
                    carried = step(first + (size - 1 - k if back else k), carried)
                return carried

            return go

        return lax.cond(same, run(plain), run(kept), carried)

    return lax.fori_loop(0, count, chunk, carried)


def scan_kernel(seg_ref, h_ref, rate_ref, c_ref, y_ref, s_ref, e_ref):
    half = first_half()
    decay = [jnp.exp(-rate_ref[n]) for n in range(STATE)]

    def plain(t, states):
        row = h_ref[t]
        return [states[n] * decay[n] + row for n in range(STATE)]

    def kept(t, states):
        keep = keep_at(seg_ref, t, half)
        row = h_ref[t]
        return [(states[n] * keep) * decay[n] + row for n in range(STATE)]

    def reading(step):
        def go(t, states):
            states = step(t, states)
            total = c_ref[0] * states[0]
            for n in range(1, STATE):
                total = total + c_ref[n] * states[n]
            y_ref[t - (BL - CTX)] = total
            return states

        return go

    states = [jnp.zeros((8, 128), f32)] * STATE
    states = chunked(seg_ref, 0, BL - CTX, plain, kept, states)
    states = chunked(seg_ref, BL - CTX, BL, reading(plain), reading(kept), states)
    joined = flag(seg_ref[2 * BL] == seg_ref[BL])
    for n in range(STATE):
        s_ref[n] = states[n]
        ends = states[n] + (joined * jnp.exp(-rate_ref[n] * BL)) * pltpu.roll(states[n], 4, 0)
        e_ref[n] = ends


def tail_kernel(
    seg_ref, use_ref, all_ref, s_ref, rate_ref, c_ref, y_ref, out_ref, start_ref, carry_ref
):
    half = first_half()
    before = seg_ref[0]
    joined = flag(seg_ref[BL] == before)
    decay = [jnp.exp(-rate_ref[n]) for n in range(STATE)]
    carry_ref[...] = jnp.zeros_like(carry_ref)

    def gather(j, _):
        @pl.when(use_ref[j] > 0)
        def _():
            for m in range(STATE // 2):
                pair = all_ref[j, 16 * m : 16 * m + 16, :].astype(f32)
                for k in range(2):
                    n = 2 * m + k
                    power = jnp.exp(-rate_ref[n] * (2 * BL))
                    carry_ref[n] = carry_ref[n] * power + pair[8 * k : 8 * k + 8]

        return 0

    lax.fori_loop(0, all_ref.shape[0], gather, 0)
    weighted = []
    for n in range(STATE):
        carried = pltpu.roll(carry_ref[n], 4, 0)
        mid = pltpu.roll(s_ref[n], 4, 0) + (joined * jnp.exp(-rate_ref[n] * BL)) * carry_ref[n]
        start = jnp.where(half, carried, mid)
        start_ref[n] = start
        weighted.append(c_ref[n] * start * jnp.exp(-rate_ref[n] * (BL - CTX + 1)))

    def step(t, parts):
        mask = jnp.where(
            half,
            flag(seg_ref[t + 1 + BL - CTX] == before),
            flag(seg_ref[BL + t + 1 + BL - CTX] == seg_ref[BL]),
        )
        total = parts[0]
        for n in range(1, STATE):
            total = total + parts[n]
        out_ref[t] = y_ref[t] + mask * total
        return [parts[n] * decay[n] for n in range(STATE)]

    lax.fori_loop(0, CTX, step, weighted, unroll=4)


def back_total_kernel(seg_ref, g_ref, rate_ref, c_ref, own_ref, out_ref):
    half = first_half()
    decay = [jnp.exp(-rate_ref[n]) for n in range(STATE)]

    def step(k, sums):
        t = CTX - 1 - k
        mask = jnp.where(
            half,
            flag(seg_ref[t + 1 + BL - CTX] == seg_ref[1]),
            flag(seg_ref[BL + t + 1 + BL - CTX] == seg_ref[BL]),
        )
        grad = mask * g_ref[t]
        return [decay[n] * (sums[n] + grad) for n in range(STATE)]

    sums = lax.fori_loop(0, CTX, step, [jnp.zeros((8, 128), f32)] * STATE, unroll=4)
    joined = flag(seg_ref[1] == seg_ref[BL])
    for n in range(STATE):
        total = sums[n] * c_ref[n] * jnp.exp(-rate_ref[n] * (BL - CTX))
        own_ref[n] = total
        out_ref[n] = total + (joined * jnp.exp(-rate_ref[n] * BL)) * pltpu.roll(total, 4, 0)


def sens_steps(seg_ref, h_ref, half, decay, count):
    def plain(t, both):
        row = h_ref[t]
        sens = [both[1][n] * decay[n] + both[0][n] for n in range(count)]
        states = [both[0][n] * decay[n] + row for n in range(count)]
        return [states, sens] + list(both[2:])

    def kept(t, both):
        keep = keep_at(seg_ref, t, half)
        row = h_ref[t]
        held = [v * keep for v in both[0]]
        sens = [(both[1][n] * keep) * decay[n] + held[n] for n in range(count)]
        states = [held[n] * decay[n] + row for n in range(count)]
        return [states, sens] + list(both[2:])

    return plain, kept


SENS_GROUP = 8


def sens_kernel(seg_ref, h_ref, start_ref, rate_ref, s_ref, z_ref):
    half = first_half()
    for first in range(0, STATE, SENS_GROUP):
        ids = range(first, first + SENS_GROUP)
        decay = [jnp.exp(-rate_ref[n]) for n in ids]
        plain, kept = sens_steps(seg_ref, h_ref, half, decay, SENS_GROUP)
        both = [[start_ref[n] for n in ids], [jnp.zeros((8, 128), f32)] * SENS_GROUP]
        both = chunked(seg_ref, 0, BL - CTX, plain, kept, both)
        for k, n in enumerate(ids):
            s_ref[n] = both[0][k]
            z_ref[n] = both[1][k]


def sens_tail_kernel(seg_ref, h_ref, g_ref, s_ref, z_ref, rate_ref, gc_ref, ga_ref, zend_ref):
    half = first_half()
    for first in range(0, STATE, SENS_GROUP):
        ids = range(first, first + SENS_GROUP)
        decay = [jnp.exp(-rate_ref[n]) for n in ids]

        def summing(step):
            def go(t, carried):
                states, sens, by_c, by_a = step(t, carried)
                grad = g_ref[t - (BL - CTX)]
                by_c = [by_c[n] + grad * states[n] for n in range(SENS_GROUP)]
                by_a = [by_a[n] + grad * sens[n] for n in range(SENS_GROUP)]
                return [states, sens, by_c, by_a]

            return go

        plain, kept = sens_steps(seg_ref, h_ref, half, decay, SENS_GROUP)
        zeros = [jnp.zeros((8, 128), f32)] * SENS_GROUP
        carried = [[s_ref[n] for n in ids], [z_ref[n] for n in ids], zeros, zeros]
        carried = chunked(seg_ref, BL - CTX, BL, summing(plain), summing(kept), carried)
        for k, n in enumerate(ids):
            zend_ref[n] = carried[1][k]
            gc_ref[n] = carried[2][k]
            ga_ref[n] = carried[3][k]


def back_scan_kernel(
    seg_ref,
    use_ref,
    all_ref,
    g_ref,
    own_ref,
    z_ref,
    ga_ref,
    rate_ref,
    c_ref,
    gh_ref,
    out_ref,
    later_ref,
):
    half = first_half()
    decay = [jnp.exp(-rate_ref[n]) for n in range(STATE)]
    joined = flag(seg_ref[2 * BL] == seg_ref[BL])
    later_ref[...] = jnp.zeros_like(later_ref)
    count = all_ref.shape[0]

    def gather(k, _):
        j = count - 1 - k

        @pl.when(use_ref[j] > 0)
        def _():
            for m in range(STATE // 2):
                pair = all_ref[j, 16 * m : 16 * m + 16, :].astype(f32)
                for k in range(2):
                    n = 2 * m + k
                    power = jnp.exp(-rate_ref[n] * (2 * BL))
                    later_ref[n] = later_ref[n] * power + pair[8 * k : 8 * k + 8]

        return 0

    lax.fori_loop(0, count, gather, 0)
    sums = []
    for n in range(STATE):
        first = (
            pltpu.roll(own_ref[n], 4, 0) + (joined * jnp.exp(-rate_ref[n] * BL)) * later_ref[n]
        )
        entering = jnp.where(half, first, pltpu.roll(later_ref[n], 4, 0))
        sums.append(entering)
        out_ref[n] = ga_ref[n] * c_ref[n] + entering * z_ref[n]

    def total_of(t, sums):
        total = sums[0]
        for n in range(1, STATE):
            total = total + sums[n]
        gh_ref[t] = total

    def plain(t, sums):
        total_of(t, sums)
        return [v * decay[n] for n, v in enumerate(sums)]

    def kept(t, sums):
        total_of(t, sums)
        keep = keep_at(seg_ref, t, half)
        return [(v * keep) * decay[n] for n, v in enumerate(sums)]

    def entered(step):
        def go(t, sums):
            grad = g_ref[t - (BL - CTX)]
            return step(t, [sums[n] + c_ref[n] * grad for n in range(STATE)])

        return go

    sums = chunked(seg_ref, BL - CTX, BL, entered(plain), entered(kept), sums, back=True)
    chunked(seg_ref, 0, BL - CTX, plain, kept, sums, back=True)


def to_lanes(values, blocks, steps):
    return (
        values.reshape(blocks, steps, 4, 128).transpose(1, 0, 2, 3).reshape(steps, blocks * 4, 128)
    )


def from_lanes(values, blocks, steps):
    return values.reshape(steps, blocks, 4, 128).transpose(1, 0, 2, 3).reshape(blocks, steps, 512)


def attend_kernel(
    host_ref,
    hid_ref,
    ctx_ref,
    wq_ref,
    wk_ref,
    wv_ref,
    segq_ref,
    segk_ref,
    q_ref,
    k_ref,
    v_ref,
    ck_ref,
    cv_ref,
    pc_ref,
    pb_ref,
    mix_ref,
):
    hid = hid_ref[...]
    ctx = ctx_ref[...]
    q_ref[...] = dot_nn(hid, wq_ref[0]).astype(bf16)
    k_ref[...] = dot_nn(hid, wk_ref[0]).astype(bf16)
    v_ref[...] = dot_nn(hid, wv_ref[0]).astype(bf16)
    ck_ref[...] = dot_nn(ctx, wk_ref[0]).astype(bf16)
    cv_ref[...] = dot_nn(ctx, wv_ref[0]).astype(bf16)
    ctx_ids = segk_ref[:, :CTX]
    for i in range(BL // QT):
        rows = slice(i * QT, (i + 1) * QT)
        reach = (i + 1) * QT
        ids = segq_ref[rows]
        ctx_ok = ctx_ids == ids
        place_q = lax.broadcasted_iota(i32, (QT, reach), 0) + i * QT
        place_k = lax.broadcasted_iota(i32, (QT, reach), 1)
        block_ok = jnp.logical_and(place_k <= place_q, segk_ref[:, CTX : CTX + reach] == ids)
        for head in range(TILE // HEAD_DIM):
            cols = slice(head * HEAD_DIM, (head + 1) * HEAD_DIM)
            query = q_ref[rows, cols]
            sc = dot_nt(query, ck_ref[:, cols]) * (score_scale * LOG2E)
            sb = dot_nt(query, k_ref[:reach, cols]) * (score_scale * LOG2E)
            sc = jnp.where(ctx_ok, sc, masked_score)
            sb = jnp.where(block_ok, sb, masked_score)
            top = jnp.maximum(
                jnp.max(sc, axis=1, keepdims=True), jnp.max(sb, axis=1, keepdims=True)
            )
            ec = jnp.exp2(sc - top)
            eb = jnp.exp2(sb - top)
            total = jnp.sum(ec, axis=1, keepdims=True) + jnp.sum(eb, axis=1, keepdims=True)
            inverse = 1.0 / total
            pc = (ec * inverse).astype(bf16)
            pb = (eb * inverse).astype(bf16)
            pc_ref[head, rows, :] = pc
            pb_ref[head, rows, :reach] = pb
            if reach < BL:
                pb_ref[head, rows, reach:] = jnp.zeros((QT, BL - reach), bf16)
            mixed = dot_nn(pc, cv_ref[:, cols]) + dot_nn(pb, v_ref[:reach, cols])
            mix_ref[rows, cols] = mixed.astype(bf16)


def attend_forward(hosts, block, hidden, context, attn_full, seg_col, seg_row, half_width):
    pairs = half_width // TILE

    def weight(position):
        return pl.BlockSpec((1, D, TILE), lambda p, s: (s[position], 0, p))

    def tile(rows):
        return pl.BlockSpec((rows, TILE), lambda p, s: (0, p))

    heads = half_width // HEAD_DIM
    per = TILE // HEAD_DIM
    return call(
        attend_kernel,
        (pairs,),
        [
            pl.BlockSpec((BL, D), lambda p, s: (block, 0)),
            pl.BlockSpec((CTX, D), lambda p, s: (block, 0)),
            weight(0),
            weight(1),
            weight(2),
            pl.BlockSpec((BL, 1), lambda p, s: (block, 0)),
            whole((1, CTX + BL)),
        ],
        [
            tile(BL),
            tile(BL),
            tile(BL),
            tile(CTX),
            tile(CTX),
            pl.BlockSpec((per, BL, CTX), lambda p, s: (p, 0, 0)),
            pl.BlockSpec((per, BL, BL), lambda p, s: (p, 0, 0)),
            tile(BL),
        ],
        [
            pltpu.HBM((BL, half_width), bf16),
            pltpu.HBM((BL, half_width), bf16),
            pltpu.HBM((BL, half_width), bf16),
            pltpu.HBM((CTX, half_width), bf16),
            pltpu.HBM((CTX, half_width), bf16),
            pltpu.HBM((heads, BL, CTX), bf16),
            pltpu.HBM((heads, BL, BL), bf16),
            sds((BL, half_width), bf16),
        ],
        prefetch=1,
        flops=8 * 10**9,
        nbytes=12 * 10**6,
    )(
        hosts,
        hbm(hidden),
        context,
        *hbm(attn_full, attn_full, attn_full),
        seg_col,
        seg_row,
    )


def attend_back_kernel(
    host_ref,
    own_ref,
    other_ref,
    cot_ref,
    mid_ref,
    gain_ref,
    tok_ref,
    first_gain_ref,
    wo_ref,
    wq_ref,
    wk_ref,
    wv_ref,
    q_ref,
    k_ref,
    v_ref,
    ck_ref,
    cv_ref,
    pc_ref,
    pb_ref,
    low_ref,
    gmid_ref,
    ggain_ref,
    dq_ref,
    dk_ref,
    dv_ref,
    dck_ref,
    dcv_ref,
    hown_ref,
    hsend_ref,
    cown_ref,
    csend_ref,
    sum_ref,
    dsc_ref,
    dsb_ref,
):
    step = pl.program_id(0)
    pairs = pl.num_programs(0) - 2

    @pl.when(step == 0)
    def _():
        grad = own_ref[...].astype(f32) + other_ref[...].astype(f32)
        middle = mid_ref[...]
        inverse = lax.rsqrt(jnp.mean(middle * middle, axis=1, keepdims=True) + epsilon_norm)
        scaled = middle * inverse
        ggain_ref[...] = jnp.sum(grad * scaled, axis=0, keepdims=True)
        weighted = grad * gain_ref[...]
        centre = jnp.mean(weighted * scaled, axis=1, keepdims=True)
        result = cot_ref[...].astype(f32) + inverse * (weighted - scaled * centre)
        gmid_ref[...] = result
        low_ref[...] = result.astype(bf16)

    @pl.when(step < pairs)
    def _():
        grad_mixed = dot_nn(low_ref[...], wo_ref[0]).astype(bf16)
        base = step * TILE
        for head in range(TILE // HEAD_DIM):
            cols = slice(head * HEAD_DIM, (head + 1) * HEAD_DIM)
            to = pl.ds(pl.multiple_of(base + head * HEAD_DIM, HEAD_DIM), HEAD_DIM)
            grad_head = grad_mixed[:, cols]
            for i in range(BL // QT):
                rows = slice(i * QT, (i + 1) * QT)
                reach = (i + 1) * QT
                grad_rows = grad_head[rows]
                gpc = dot_nt(grad_rows, cv_ref[:, cols])
                gpb = dot_nt(grad_rows, v_ref[:reach, cols])
                pc = pc_ref[head, rows, :].astype(f32)
                pb = pb_ref[head, rows, :reach].astype(f32)
                tc = pc * gpc
                tb = pb * gpb
                centre = jnp.sum(tc, axis=1, keepdims=True) + jnp.sum(tb, axis=1, keepdims=True)
                dsc_ref[head, rows, :] = (tc - pc * centre).astype(bf16)
                dsb_ref[head, rows, :reach] = (tb - pb * centre).astype(bf16)
                if reach < BL:
                    dsb_ref[head, rows, reach:] = jnp.zeros((QT, BL - reach), bf16)
            dsc = dsc_ref[head]
            dsb = dsb_ref[head]
            dq = (dot_nn(dsc, ck_ref[:, cols]) + dot_nn(dsb, k_ref[:, cols])) * score_scale
            dq_ref[:, to] = dq.astype(bf16)
            query = q_ref[:, cols]
            dk_ref[:, to] = (dot_tn(dsb, query) * score_scale).astype(bf16)
            dck_ref[:, to] = (dot_tn(dsc, query) * score_scale).astype(bf16)
            dv_ref[:, to] = dot_tn(pb_ref[head], grad_head).astype(bf16)
            dcv_ref[:, to] = dot_tn(pc_ref[head], grad_head).astype(bf16)

    def half():
        part = (
            dot_nt(dq_ref[...], wq_ref[0])
            + dot_nt(dk_ref[...], wk_ref[0])
            + dot_nt(dv_ref[...], wv_ref[0])
        )
        ctx_part = dot_nt(dck_ref[...], wk_ref[0]) + dot_nt(dcv_ref[...], wv_ref[0])
        row_sum = jnp.sum(
            part * (tok_ref[...].astype(f32) * first_gain_ref[...]), axis=1, keepdims=True
        )
        return part, ctx_part, row_sum

    @pl.when(step == pairs)
    def _():
        part, ctx_part, row_sum = half()
        hsend_ref[...] = part.astype(bf16)
        csend_ref[...] = ctx_part.astype(bf16)
        sum_ref[...] = row_sum

    @pl.when(step == pairs + 1)
    def _():
        part, ctx_part, row_sum = half()
        hown_ref[...] = part
        cown_ref[...] = ctx_part
        sum_ref[...] += row_sum


def attend_backward(
    hosts, block, own, other, cot_full, middle, gain, tok_full, first_gain, attn_full, kept, width
):
    pairs = width // TILE
    per = TILE // HEAD_DIM

    def pair(p):
        return jnp.minimum(p, pairs - 1)

    def side(p, s):
        return jnp.where(p <= pairs, 1 - s[8], s[8])

    def weight(position):
        return pl.BlockSpec((1, width, width), lambda p, s: (s[position], side(p, s), 0))

    def tile(rows):
        return pl.BlockSpec((rows, TILE), lambda p, s: (0, pair(p)))

    return call(
        attend_back_kernel,
        (pairs + 2,),
        [
            whole((BL, D)),
            whole((BL, D)),
            pl.BlockSpec((BL, D), lambda p, s: (block, 0)),
            whole((BL, D)),
            whole((1, D)),
            pl.BlockSpec((BL, width), lambda p, s: (block, side(p, s))),
            pl.BlockSpec((1, width), lambda p, s: (0, side(p, s))),
            pl.BlockSpec((1, D, TILE), lambda p, s: (s[3], 0, pair(p))),
            weight(0),
            weight(1),
            weight(2),
            tile(BL),
            tile(BL),
            tile(BL),
            tile(CTX),
            tile(CTX),
            pl.BlockSpec((per, BL, CTX), lambda p, s: (pair(p), 0, 0)),
            pl.BlockSpec((per, BL, BL), lambda p, s: (pair(p), 0, 0)),
        ],
        [
            whole((BL, D)),
            whole((BL, D)),
            whole((1, D)),
            whole((BL, width)),
            whole((BL, width)),
            whole((BL, width)),
            whole((CTX, width)),
            whole((CTX, width)),
            whole((BL, width)),
            whole((BL, width)),
            whole((CTX, width)),
            whole((CTX, width)),
            whole((BL, 1)),
        ],
        [
            pltpu.HBM((BL, D), bf16),
            pltpu.HBM((BL, D), f32),
            sds((1, D), f32),
            pltpu.HBM((BL, width), bf16),
            pltpu.HBM((BL, width), bf16),
            pltpu.HBM((BL, width), bf16),
            pltpu.HBM((CTX, width), bf16),
            pltpu.HBM((CTX, width), bf16),
            pltpu.HBM((BL, width), f32),
            sds((BL, width), bf16),
            sds((CTX, width), f32),
            sds((CTX, width), bf16),
            sds((BL, 1), f32),
        ],
        scratch=[pltpu.VMEM((per, BL, CTX), bf16), pltpu.VMEM((per, BL, BL), bf16)],
        prefetch=1,
        flops=12 * 10**9,
        nbytes=20 * 10**6,
    )(
        hosts,
        *hbm(own, other, cot_full, middle),
        gain,
        hbm(tok_full),
        first_gain,
        *hbm(attn_full, attn_full, attn_full, attn_full, *kept),
    )


def attn_grad_kernel(host_ref, *refs):
    (hid0, hid1, ctx0, ctx1, low0, low1), rest = refs[:6], refs[6:]
    (dq0, dk0, dv0, dck0, dcv0, mix0), rest = rest[:6], rest[6:]
    (dq1, dk1, dv1, dck1, dcv1, mix1), (out_ref,) = rest[:6], rest[6:]
    matrix = pl.program_id(0)

    @pl.when(matrix == 0)
    def _():
        out_ref[0] = (dot_tn(hid0[...], dq0[...]) + dot_tn(hid1[...], dq1[...])).astype(bf16)

    @pl.when(matrix == 1)
    def _():
        out_ref[0] = (
            dot_tn(hid0[...], dk0[...])
            + dot_tn(hid1[...], dk1[...])
            + dot_tn(ctx0[...], dck0[...])
            + dot_tn(ctx1[...], dck1[...])
        ).astype(bf16)

    @pl.when(matrix == 2)
    def _():
        out_ref[0] = (
            dot_tn(hid0[...], dv0[...])
            + dot_tn(hid1[...], dv1[...])
            + dot_tn(ctx0[...], dcv0[...])
            + dot_tn(ctx1[...], dcv1[...])
        ).astype(bf16)

    @pl.when(matrix == 3)
    def _():
        out_ref[0] = (dot_tn(low0[...], mix0[...]) + dot_tn(low1[...], mix1[...])).astype(bf16)


def attn_grads(hosts, hidden, context, lows, blocks, half_width):
    hid_specs = [
        pl.BlockSpec((BL, D), lambda m, s: (0, 0)),
        pl.BlockSpec((BL, D), lambda m, s: (1, 0)),
        pl.BlockSpec((CTX, D), lambda m, s: (0, 0)),
        pl.BlockSpec((CTX, D), lambda m, s: (1, 0)),
    ]
    block_specs = [
        whole((BL, half_width)),
        whole((BL, half_width)),
        whole((BL, half_width)),
        whole((CTX, half_width)),
        whole((CTX, half_width)),
        whole((BL, half_width)),
    ]
    return call(
        attn_grad_kernel,
        (4,),
        hid_specs + [whole((BL, D))] * 2 + block_specs * 2,
        [pl.BlockSpec((1, D, half_width), lambda m, s: (s[m], 0, 0))],
        [pltpu.HBM((OWNER_GROUPS, D, half_width), bf16)],
        prefetch=1,
        flops=46 * 10**8,
        nbytes=14 * 10**6,
    )(hosts, *hbm(hidden, hidden, context, context, *lows, *blocks[0], *blocks[1]))[0]


def mlp_kernel(
    host_ref,
    own_ref,
    other_ref,
    wo_ref,
    woo_ref,
    tok_ref,
    gain_ref,
    cot_ref,
    w1_ref,
    w2_ref,
    mid_ref,
    hid_ref,
    act_ref,
    pre_ref,
    low_ref,
    grad_ref,
):
    step = pl.program_id(0)

    @pl.when(step == 0)
    def _():
        middle = (
            tok_ref[...].astype(f32)
            + dot_nt(own_ref[...], wo_ref[0])
            + dot_nt(other_ref[...], woo_ref[...])
        )
        inverse = lax.rsqrt(jnp.mean(middle * middle, axis=1, keepdims=True) + epsilon_norm)
        mid_ref[...] = middle
        hid_ref[...] = (middle * inverse * gain_ref[...]).astype(bf16)
        grad_ref[...] = jnp.zeros_like(grad_ref)

    w1 = w1_ref[0]
    w2 = w2_ref[0]
    pre = dot_nn(hid_ref[...], w1)
    grad_act = dot_nn(cot_ref[...], w2)
    root = 0.7978845608028654
    square = pre * pre
    gate = 0.5 + 0.5 * jnp.tanh(pre * (root + (root * 0.044715) * square))
    act = pre * gate
    act_ref[...] = act.astype(bf16)
    slope = gate + act * (1.0 - gate) * (2.0 * root + (6.0 * root * 0.044715) * square)
    grad_pre = (slope * grad_act).astype(bf16)
    pre_ref[...] = grad_pre
    grad_ref[...] += dot_nt(grad_pre, w1)

    @pl.when(step == pl.num_programs(0) - 1)
    def _():
        low_ref[...] = grad_ref[...].astype(bf16)


def mlp_block(hosts, block, own, other, attn_full, wo_other, tok_full, gain, cot_full, mlp_full):
    half_width = own.shape[1]
    quarter = mlp_full.shape[2]
    hidden = 2 * quarter
    per = quarter // FT

    def weight(position):
        return pl.BlockSpec(
            (1, D, FT), lambda f, s: (s[4 + 2 * position + f // per], 0, lax.rem(f, per))
        )

    return call(
        mlp_kernel,
        (2 * per,),
        [
            whole((BL, half_width)),
            whole((BL, half_width)),
            pl.BlockSpec((1, D, half_width), lambda f, s: (s[3], 0, 0)),
            whole((D, half_width)),
            pl.BlockSpec((BL, D), lambda f, s: (block, 0)),
            whole((1, D)),
            pl.BlockSpec((BL, D), lambda f, s: (block, 0)),
            weight(0),
            weight(1),
        ],
        [
            whole((BL, D)),
            whole((BL, D)),
            pl.BlockSpec((BL, FT), lambda f, s: (0, f)),
            pl.BlockSpec((BL, FT), lambda f, s: (0, f)),
            whole((BL, D)),
        ],
        [
            pltpu.HBM((BL, D), f32),
            sds((BL, D), bf16),
            pltpu.HBM((BL, hidden), bf16),
            sds((BL, hidden), bf16),
            pltpu.HBM((BL, D), bf16),
        ],
        scratch=[pltpu.VMEM((BL, D), f32)],
        prefetch=1,
        flops=8 * 10**9,
        nbytes=24 * 10**6,
    )(
        hosts,
        own,
        other,
        hbm(attn_full),
        wo_other,
        tok_full,
        gain,
        cot_full,
        *hbm(mlp_full, mlp_full),
    )


def mlp_grad_kernel(host_ref, h0, h1, g0, g1, p0, p1, a0, a1, out_ref):
    matrix = pl.program_id(0)

    @pl.when(matrix == 0)
    def _():
        out_ref[0] = (dot_tn(h0[...], p0[...]) + dot_tn(h1[...], p1[...])).astype(bf16)

    @pl.when(matrix == 1)
    def _():
        out_ref[0] = (dot_tn(g0[...], a0[...]) + dot_tn(g1[...], a1[...])).astype(bf16)


def mlp_grads(hosts, hiddens, cot_full, pres, acts):
    hidden = acts[0].shape[1]
    quarter = hidden // 2
    per = quarter // FT
    last = 2 * per - 1
    used_first = pl.BlockSpec((BL, FT), lambda m, f, s: (0, jnp.where(m == 0, f, last)))
    used_second = pl.BlockSpec((BL, FT), lambda m, f, s: (0, jnp.where(m == 1, f, 0)))
    return call(
        mlp_grad_kernel,
        (2, 2 * per),
        [
            whole((BL, D)),
            whole((BL, D)),
            pl.BlockSpec((BL, D), lambda m, f, s: (0, 0)),
            pl.BlockSpec((BL, D), lambda m, f, s: (1, 0)),
            used_first,
            used_first,
            used_second,
            used_second,
        ],
        [
            pl.BlockSpec(
                (1, D, FT), lambda m, f, s: (s[4 + 2 * m + f // per], 0, lax.rem(f, per))
            )
        ],
        [pltpu.HBM((OWNER_GROUPS, D, quarter), bf16)],
        prefetch=1,
        flops=86 * 10**8,
        nbytes=20 * 10**6,
    )(
        hosts,
        hiddens[0],
        hiddens[1],
        cot_full,
        cot_full,
        *pres,
        *acts,
    )[0]


def mlp_out_kernel(host_ref, a0, a1, wa_ref, wb_ref, mid0, mid1, send_ref, own_ref):
    step = pl.program_id(0)
    quarter = wa_ref.shape[2]

    def rows(a_ref):
        return dot_nt(a_ref[:, :quarter], wa_ref[0]) + dot_nt(a_ref[:, quarter:], wb_ref[0])

    @pl.when(step == 0)
    def _():
        send_ref[:BL, :] = rows(a0).astype(bf16)
        send_ref[BL:, :] = rows(a1).astype(bf16)

    @pl.when(step == 1)
    def _():
        own_ref[:BL, :] = rows(a0) + mid0[...]
        own_ref[BL:, :] = rows(a1) + mid1[...]


def mlp_out(hosts, acts, mlp_full, middles, width):
    quarter = mlp_full.shape[2]

    def side(d, s):
        return jnp.where(d == 0, 1 - s[8], s[8])

    def weight(position):
        return pl.BlockSpec((1, width, quarter), lambda d, s: (s[position], side(d, s), 0))

    middle = pl.BlockSpec((BL, width), lambda d, s: (0, s[8]))
    return call(
        mlp_out_kernel,
        (2,),
        [whole((BL, 2 * quarter))] * 2 + [weight(6), weight(7), middle, middle],
        [whole((2 * BL, width))] * 2,
        [sds((2 * BL, width), bf16), pltpu.HBM((2 * BL, width), f32)],
        prefetch=1,
        flops=44 * 10**8,
        nbytes=12 * 10**6,
    )(hosts, *hbm(*acts, mlp_full, mlp_full, *middles))


def adam_step(gradient, moment_one, moment_two, weight, rate_table, decay_weight):
    step_count = f32(STEP)
    first_new = beta_first * moment_one + (1.0 - beta_first) * gradient
    second_new = beta_second * moment_two + (1.0 - beta_second) * gradient * gradient
    fixed_one = 1.0 - jnp.power(beta_first, step_count)
    fixed_two = 1.0 - jnp.power(beta_second, step_count)
    update = first_new / fixed_one / (jnp.sqrt(second_new / fixed_two) + epsilon_adam)
    return (first_new, second_new, weight - rate_table * (update + decay_weight * weight))


def body(
    tokens,
    cotangent,
    segments,
    owners,
    attn_master,
    attn_first,
    attn_second,
    mlp_master,
    mlp_first,
    mlp_second,
    ssm_params,
    ssm_first,
    ssm_second,
    norm_gains,
    gains_first,
    gains_second,
):
    rows = tokens.shape[1]
    width = tokens.shape[2]
    blocks = rows // BL
    dp_count = lax.axis_size("dp")
    dp_here = lax.axis_index("dp")
    side = lax.axis_index("tensor")
    group = dp_here // (dp_count // OWNER_GROUPS)
    quarter = mlp_master.shape[2] // 2

    def both_sides(own, other):
        return jnp.where(
            side == 0,
            jnp.concatenate([own, other], axis=-1),
            jnp.concatenate([other, own], axis=-1),
        )

    def side_of(values, which):
        return lax.dynamic_slice_in_dim(values, which * width, width, values.ndim - 1)

    smem = pl.BlockSpec(memory_space=pltpu.SMEM)
    vmem = pl.BlockSpec(memory_space=pltpu.VMEM)
    hosts, rates = pl.pallas_call(
        plan_kernel,
        in_specs=[smem, smem],
        out_specs=[smem, smem],
        out_shape=[sds((PLAN_SIZE,), i32), sds((4,), f32)],
    )(owners, jnp.stack([side, group]).astype(i32))
    attn_here = hosts[ATTN_HERE]
    mlp_here = hosts[MLP_HERE]
    near = hosts[NEAR] == 1
    ring = Ring()

    tok = tokens.reshape(rows, width)
    cot = cotangent.reshape(rows, width)
    tok_f = tok.astype(f32)
    square_here = jnp.sum(tok_f * tok_f, axis=1)
    square_other = swap_x(square_here)
    tok_other = swap_x(tok)
    gains_other = swap_x(norm_gains)
    inverse_one = lax.rsqrt((square_here + square_other) / D + epsilon_norm)
    scaled_own = tok_f * inverse_one[:, None]
    hidden_own = (scaled_own * norm_gains[0]).astype(bf16)
    gains_full = both_sides(norm_gains, gains_other)

    attn_low = attn_master.astype(bf16)
    mlp_low = mlp_master[0].astype(bf16)
    attn_moved = move(attn_low[1], hosts[WAY], ATTN_WAYS, False)
    attn_block = jnp.where(attn_here == 0, attn_moved, attn_low[0])
    attn_full = lax.all_gather(attn_block, "dp", axis=0, tiled=True)
    attn_full = attn_full.reshape(OWNER_GROUPS, D, width)
    mlp_moved = exchange_groups(gate(mlp_low[:, quarter:], square_other), near)

    seg = segments.reshape(rows)
    prior = lax.ppermute(seg[rows - CTX :] + 1, "dp", [(i, i + 1) for i in range(dp_count - 1)]) - 1
    seg_ext = jnp.concatenate([prior[CTX - 1 :], seg])
    seg_col = seg[:, None]

    param_lanes = ssm_params.transpose(0, 2, 1)
    decay_rate = jnp.exp(param_lanes[0]) * (BL ** (-0.5) / 32.0)
    drive_root = jnp.sqrt(-jnp.expm1(-2.0 * decay_rate))
    reading = param_lanes[2] * drive_root * param_lanes[1]

    def doubled(values):
        lanes = values.reshape(STATE, 4, 128)
        return jnp.concatenate([lanes] * blocks, axis=1)

    rate_lanes = doubled(decay_rate)
    reading_lanes = doubled(reading)
    state_shape = sds((STATE, 8, 128), f32)

    def plain(kernel, scalars, count, outs, cost, scratch=()):
        return pl.pallas_call(
            kernel,
            in_specs=[smem] * scalars + [vmem] * count,
            out_specs=[vmem] * len(outs),
            out_shape=outs,
            scratch_shapes=scratch,
            name=kernel.__name__,
            compiler_params=pltpu.CompilerParams(vmem_limit_bytes=16 * 1024 * 1024),
            cost_estimate=pl.CostEstimate(flops=cost // COST, bytes_accessed=10**6 // COST, transcendentals=0),
        )

    hidden_lanes = to_lanes(hidden_own.astype(f32), blocks, BL)
    tail_lanes = sds((CTX, 8, 128), f32)
    tail_part, state_ends, device_end = plain(
        scan_kernel, 1, 3, [tail_lanes, state_shape, state_shape], 4 * 10**9
    )(seg_ext, hidden_lanes, rate_lanes, reading_lanes)
    id_rows = jnp.where(
        (jnp.arange(16) == 0)[:, None], seg[rows - 1].astype(f32), seg[0].astype(f32)
    )
    message = jnp.concatenate(
        [device_end.reshape(STATE * 8, 128), jnp.broadcast_to(id_rows, (16, 128))], axis=0
    ).astype(bf16)
    hidden_full = join_sides(
        hosts,
        tok,
        tok_other,
        (inverse_one[:, None], norm_gains[0:1], gains_other[0:1]),
    )
    states_all = gather_round(message[None], 0)
    cot_other = swap_x(gate(cot, tok_other))
    for k in range(1, gather_rounds()):
        if k == gather_rounds() - 2:
            tok_other, states_all = together(tok_other, states_all)
        if k == gather_rounds() - 1:
            mlp_moved, states_all = together(mlp_moved, states_all)
        states_all = gather_round(states_all, k)
    states_all = gate(states_all, cot_other, hidden_full)
    mlp_block_low = jnp.where(mlp_here == 0, mlp_moved, mlp_low[:, :quarter])
    mlp_full = lax.all_gather(mlp_block_low, "dp", axis=0, tiled=True)
    mlp_full = mlp_full.reshape(OWNER_GROUPS, D, quarter)
    tok_full = join_sides(hosts, tok, tok_other)
    ids_all = states_all[:, STATE * 8 : STATE * 8 + 2, 0].astype(i32)
    places = jnp.arange(dp_count, dtype=i32)
    use_before = jnp.logical_and(places < dp_here, ids_all[:, 0] == seg_ext[0]).astype(i32)
    use_after = jnp.logical_and(places > dp_here, ids_all[:, 1] == seg[rows - 1]).astype(i32)
    tails, state_starts = plain(
        tail_kernel, 2, 5, [tail_lanes, state_shape], 10**9, [pltpu.VMEM((STATE, 8, 128), f32)]
    )(seg_ext, use_before, states_all, state_ends, rate_lanes, reading_lanes, tail_part)
    sens_states, sens_starts = plain(sens_kernel, 1, 3, [state_shape] * 2, 6 * 10**9)(
        seg_ext, hidden_lanes, state_starts, rate_lanes
    )
    tails = from_lanes(tails, blocks, CTX).astype(bf16)
    context_own = shift_tails(tails[blocks - 1], 1, False)
    context_other = shift_tails(tails[blocks - 1], 1, True)
    inner_own = tails[: blocks - 1]
    inner_other = swap_x(inner_own)
    context_full = jnp.concatenate(
        [
            both_sides(context_own, context_other)[None],
            both_sides(inner_own, inner_other),
        ],
        axis=0,
    ).reshape(-1, D)

    seg_rows = []
    for b in range(blocks):
        before = prior if b == 0 else seg[b * BL - CTX : b * BL]
        seg_rows.append(jnp.concatenate([before, seg[b * BL : (b + 1) * BL]])[None])
    kept = []
    mixed = []
    mixed_other = []
    for b in range(blocks):
        outs = attend_forward(
            hosts, b, hidden_full, context_full, attn_full, seg_col, seg_rows[b], width
        )
        kept.append(outs[:7])
        mixed.append(outs[7])
        mixed_other.append(swap_x(outs[7]))
    wo_own = lax.dynamic_index_in_dim(attn_full, hosts[3], 0, keepdims=False)
    wo_half = lax.dynamic_slice_in_dim(wo_own, ring.core * (D // 2), D // 2, 0)
    wo_half = gate(wo_half, inner_other)
    wo_first = swap_x(wo_half)
    wo_second = lax.ppermute(gate(wo_first, mixed[0]), "dp", ring.cores)
    joined = together(*mixed_other, sens_states, sens_starts)
    mixed_other, (sens_states, sens_starts) = list(joined[:blocks]), joined[blocks:]
    wo_other = jnp.where(
        ring.core == 0,
        jnp.concatenate([wo_first, wo_second], axis=0),
        jnp.concatenate([wo_second, wo_first], axis=0),
    )

    cot_full = join_sides(hosts, gate(cot, mixed[0]), cot_other)

    gain_two = gains_full[1:2]
    middles, hiddens, acts, pres, grads, grads_other = [], [], [], [], [], []
    for b in range(blocks):
        middle, hidden_two, act, grad_pre, grad_low = mlp_block(
            hosts,
            b,
            mixed[b],
            mixed_other[b],
            attn_full,
            wo_other,
            tok_full,
            gain_two,
            cot_full,
            mlp_full,
        )
        middles.append(middle)
        hiddens.append(hidden_two)
        acts.append(act)
        pres.append(grad_pre)
        grads.append(grad_low)
        grads_other.append(swap_x(grad_low))
    mlp_sum_in = mlp_grads(hosts, hiddens, cot_full, pres, acts)
    grads_other[0], mlp_sum_in = lax.optimization_barrier((grads_other[0], mlp_sum_in))
    mlp_sum = lax.psum_scatter(
        mlp_sum_in.reshape(OWNER_GROUPS * D, quarter), "dp", scatter_dimension=0, tiled=True
    )

    lows, grad_mids, gain_twos, grad_blocks = [], [], [], []
    parts, parts_sent, ctx_parts, ctx_sent, row_sums = [], [], [], [], []
    for b in range(blocks):
        if b == blocks - 1:
            acts[0] = gate(acts[0], *lows)
            out_send, out_own = mlp_out(hosts, acts, mlp_full, middles, width)
            out_received = swap_x(out_send)
            grads[b] = gate(grads[b], out_own)
        outs = attend_backward(
            hosts,
            b,
            gate(grads[b], *lows),
            grads_other[b],
            cot_full,
            middles[b],
            gain_two,
            tok_full,
            gains_full[0:1],
            attn_full,
            kept[b],
            width,
        )
        lows.append(outs[0])
        grad_mids.append(side_of(outs[1], side))
        gain_twos.append(side_of(outs[2], side))
        grad_blocks.append(list(outs[3:8]) + [mixed[b]])
        parts.append(outs[8])
        parts_sent.append(outs[9])
        ctx_parts.append(outs[10])
        ctx_sent.append(outs[11])
        row_sums.append(outs[12][:, 0])
    grad_tails = jnp.stack(
        [ctx_parts[b] + swap_x(ctx_sent[b]).astype(f32) for b in range(1, blocks)]
        + [
            shift_tails(ctx_parts[0].astype(bf16), -1, False).astype(f32)
            + shift_tails(ctx_sent[0], -1, True).astype(f32)
        ]
    )
    tail_grad_lanes = to_lanes(grad_tails.reshape(blocks * CTX, width), blocks, CTX)
    own_back, device_back = plain(back_total_kernel, 1, 3, [state_shape, state_shape], 10**9)(
        seg_ext, tail_grad_lanes, rate_lanes, reading_lanes
    )
    back_all = gather_round(device_back.reshape(STATE * 8, 128).astype(bf16)[None], 0)
    lows[0] = gate(lows[0], back_all)
    attn_sum_in = attn_grads(hosts, hidden_full, context_full, lows, grad_blocks, width)
    received = [swap_x(v) for v in parts_sent]
    for k in range(1, gather_rounds()):
        if k == 2:
            back_all, attn_sum_in = together(back_all, attn_sum_in)
        back_all = gather_round(back_all, k)
    part, up, down = ring.start(attn_sum_in.reshape(dp_count, -1, width))
    up, down, back_all = together(up, down, back_all)
    grad_c_lanes, grad_a_lanes, sens_end = plain(
        sens_tail_kernel, 1, 5, [state_shape] * 3, 2 * 10**9
    )(seg_ext, hidden_lanes, tail_grad_lanes, sens_states, sens_starts, rate_lanes)
    grad_lanes, grad_a_lanes = plain(
        back_scan_kernel,
        2,
        7,
        [sds((BL, 8, 128), f32), state_shape],
        4 * 10**9,
        [pltpu.VMEM((STATE, 8, 128), f32)],
    )(
        seg_ext,
        use_after,
        back_all,
        tail_grad_lanes,
        own_back,
        sens_end,
        grad_a_lanes,
        rate_lanes,
        reading_lanes,
    )
    for k in range(ring.far_up):
        if k == 1:
            up, down = together(up, down, grad_lanes)[:2]
        up, down = ring.step(k, part, up, down)
    attn_sum = (part(0) + up.astype(f32) + down.astype(f32)).astype(bf16)
    grad_channels = lax.optimization_barrier(
        from_lanes(grad_lanes, blocks, BL).reshape(rows, width)
    )

    part_own = jnp.concatenate(parts, axis=0)
    received = jnp.concatenate(received, axis=0)
    row_here = inverse_one * jnp.concatenate(row_sums) + jnp.sum(
        grad_channels * (scaled_own * norm_gains[0]), axis=1
    )
    row_other = swap_x(row_here)
    row_total = row_here + row_other
    block_out = (out_own + out_received.astype(f32)).astype(bf16)
    grad_hidden = part_own + received.astype(f32) + grad_channels
    grad_tokens = jnp.concatenate(grad_mids, axis=0) + inverse_one[:, None] * (
        grad_hidden * norm_gains[0] - scaled_own * (row_total / D)[:, None]
    )
    gain_one = jnp.sum(grad_hidden * scaled_own, axis=0)
    gain_two_sum = sum(gain_twos)[0]

    def merged(values):
        return sum(values[:, 4 * b : 4 * b + 4] for b in range(blocks)).reshape(STATE, width)

    small = jnp.concatenate(
        [merged(grad_c_lanes), merged(grad_a_lanes), gain_one[None], gain_two_sum[None]], axis=0
    )
    small, mlp_sum = together(small, mlp_sum)
    mlp_back = exchange_groups(mlp_sum, near)
    small, mlp_back = total_dp(small, mlp_back)
    grad_c, grad_a = small[:STATE], small[STATE : 2 * STATE]
    gains_grad = small[2 * STATE :]
    decay_step = jnp.exp(-decay_rate)
    grad_read = grad_c * drive_root * param_lanes[1]
    grad_drive = grad_c * drive_root * param_lanes[2]
    grad_a = grad_a - grad_c * param_lanes[1] * param_lanes[2] * decay_step / drive_root
    grad_log = -decay_rate * decay_step * grad_a
    ssm_grad = jnp.stack([grad_log, grad_drive, grad_read]).transpose(0, 2, 1)

    attn_back = move(gate(attn_sum, small), hosts[WAY], ATTN_WAYS, True)
    attn_grad = jnp.stack(
        [
            jnp.where(attn_here >= 1, attn_sum.astype(f32), 0.0),
            jnp.where(attn_here == 2, attn_back.astype(f32), 0.0),
        ]
    )
    mlp_grad = jnp.where(
        mlp_here == 1, jnp.concatenate([mlp_sum, mlp_back], axis=1).astype(f32), 0.0
    )[None]

    attn_rates = rates[:2, None, None]
    mlp_rates = rates[2]
    ssm_rates = jnp.asarray([1.0, 0.8, 0.25], f32)[:, None, None]
    gain_rates = jnp.asarray([0.6, 0.6], f32)[:, None]
    attn_one, attn_two, attn_new = adam_step(
        attn_grad, attn_first, attn_second, attn_master, attn_rates, matrix_decay
    )
    mlp_one, mlp_two, mlp_new = adam_step(
        mlp_grad, mlp_first, mlp_second, mlp_master, mlp_rates, matrix_decay
    )
    ssm_one, ssm_two, ssm_new = adam_step(
        ssm_grad, ssm_first, ssm_second, ssm_params, ssm_rates, 0.0
    )
    gain_first_new, gain_second_new, gains_new = adam_step(
        gains_grad, gains_first, gains_second, norm_gains, gain_rates, 0.0
    )
    return (
        block_out.reshape(tokens.shape),
        grad_tokens.reshape(tokens.shape),
        attn_grad,
        attn_one,
        attn_two,
        attn_new,
        attn_new.astype(bf16),
        mlp_grad,
        mlp_one,
        mlp_two,
        mlp_new,
        mlp_new.astype(bf16),
        ssm_grad,
        ssm_one,
        ssm_two,
        ssm_new,
        gains_grad,
        gain_first_new,
        gain_second_new,
        gains_new,
    )


def solution(mesh):
    in_specs = (
        P(None, "dp", "tensor"),
        P(None, "dp", "tensor"),
        P(None, "dp"),
        P(),
        P(None, "dp", "tensor"),
        P(None, "dp", "tensor"),
        P(None, "dp", "tensor"),
        P(None, "dp", "tensor"),
        P(None, "dp", "tensor"),
        P(None, "dp", "tensor"),
        P(None, "tensor", None),
        P(None, "tensor", None),
        P(None, "tensor", None),
        P(None, "tensor"),
        P(None, "tensor"),
        P(None, "tensor"),
    )
    out_specs = (
        P(None, "dp", "tensor"),
        P(None, "dp", "tensor"),
        P(None, "dp", "tensor"),
        P(None, "dp", "tensor"),
        P(None, "dp", "tensor"),
        P(None, "dp", "tensor"),
        P(None, "dp", "tensor"),
        P(None, "dp", "tensor"),
        P(None, "dp", "tensor"),
        P(None, "dp", "tensor"),
        P(None, "dp", "tensor"),
        P(None, "dp", "tensor"),
        P(None, "tensor", None),
        P(None, "tensor", None),
        P(None, "tensor", None),
        P(None, "tensor", None),
        P(None, "tensor"),
        P(None, "tensor"),
        P(None, "tensor"),
        P(None, "tensor"),
    )
    return jax.shard_map(body, mesh=mesh, in_specs=in_specs, out_specs=out_specs, check_vma=False)
```

profile of v0, /device:TPU:0, one launch (start us, length us, event | category | flops | bytes accessed | tf_op | source)
XLA Modules:
  0.0 458.3 jit_solution(9118359780648721232)
XLA Ops:
  14.1 10.5 %conditional.5 = (bf16[256,512]{1,0:T(8,128)(2,1)}) conditional(s32[]{:T(128)} %bitcast.26, bf16[256,512]{1,0:T(8,128)(2,1)S(1)} %slice_bitcast_fusion.1, bf16[256,512]{1,0:T(8,128)(2,1)S(1)} %slice_bitcast_fusion.1, bf16[256,512]{1,0:T(8,128)(2,1)S(1)} %slice_bitcast_fusion.1, ...), branch_computations={%region_1.2_spmd, %region_2.3_spmd, %region_3.4_spmd, %region_4.5_... | conditional | bytes 1048624 | solution.py:221
  14.2 5.7 %collective-permute-start = (bf16[256,512]{1,0:T(8,128)(2,1)S(1)}, bf16[256,512]{1,0:T(8,128)(2,1)}, u32[]{:S(2)}, u32[]{:S(2)}) collective-permute-start(bf16[256,512]{1,0:T(8,128)(2,1)S(1)} %param), channel_id=1, source_target_pairs={{0,8},{2,10},{4,12},{6,14},{1,9},{3,11},{5,13},{7,15}} | collective-permute-start | bytes 786440 | tf_op jit(solution)/shard_map/cond/branch_0_fun/ppermute | solution.py:219
  19.8 4.8 %collective-permute-done = bf16[256,512]{1,0:T(8,128)(2,1)} collective-permute-done((bf16[256,512]{1,0:T(8,128)(2,1)S(1)}, bf16[256,512]{1,0:T(8,128)(2,1)}, u32[]{:S(2)}, u32[]{:S(2)}) %collective-permute-start) | collective-permute-done | bytes 262176 | tf_op jit(solution)/shard_map/cond/branch_0_fun/ppermute | solution.py:219
  24.6 1.7 fusion.33
  34.3 1.6 reshape.453
  38.1 3.3 collective-permute-start.40
  41.6 3.6 fusion.17
  45.2 4.6 %scan_kernel.1 = (f32[128,8,128]{2,1,0:T(8,128)S(1)}, f32[16,8,128]{2,1,0:T(8,128)S(1)}, f32[16,8,128]{2,1,0:T(8,128)S(1)}) custom-call(s32[1025]{0:T(1024)S(1)} %pad_add_fusion.seg_ref, f32[512,8,128]{2,1,0:T(8,128)S(1)} %bitcast.196, f32[16,8,128]{2,1,0:T(8,128)S(1)} %get-tuple-element.354.rate_ref, f32[16,8,128]{2,1,0:T(8,128)S(1)} %get-tuple-element.355.c_ref), custom_call_target="tpu_custom_call" | custom-call | flops 4000000 | bytes 1000 | tf_op jit(solution)/shard_map/scan_kernel/pallas_call | solution.py:1309
  54.9 2.5 collective-permute-done.43
  58.9 6.8 %collective-permute-done.40 = bf16[256,1024]{1,0:T(8,128)(2,1)} collective-permute-done((bf16[256,1024]{1,0:T(8,128)(2,1)}, bf16[256,1024]{1,0:T(8,128)(2,1)}, u32[]{:S(2)}, u32[]{:S(2)}) %collective-permute-start.40) | collective-permute-done | bytes 524320 | tf_op jit(solution)/shard_map/ppermute | solution.py:228
  65.8 14.6 %collective-permute-done.41 = bf16[256,1024]{1,0:T(8,128)(2,1)} collective-permute-done((bf16[256,1024]{1,0:T(8,128)(2,1)}, bf16[256,1024]{1,0:T(8,128)(2,1)}, u32[]{:S(2)}, u32[]{:S(2)}) %collective-permute-start.41) | collective-permute-done | bytes 524320 | tf_op jit(solution)/shard_map/ppermute | solution.py:228
  86.4 23.1 %collective-permute-done.38 = f32[2,512]{1,0:T(2,128)S(1)} collective-permute-done((f32[2,512]{1,0:T(2,128)S(1)}, f32[2,512]{1,0:T(2,128)S(1)}, u32[]{:S(2)}, u32[]{:S(2)}) %collective-permute-start.38) | collective-permute-done | bytes 4128 | tf_op jit(solution)/shard_map/ppermute | solution.py:83
  110.5 3.6 join_scaled_kernel.1.hid_ref.refs_0_.refs_1_
  119.6 1.8 tail_kernel.1
  128.0 1.9 collective-permute-start.47
  129.9 3.1 collective-permute-start.48
  133.0 2.0 dynamic-slice_bitcast_fusion.1
  139.1 9.4 %attend_kernel.3 = (bf16[512,512]{1,0:T(8,128)(2,1)}, bf16[512,512]{1,0:T(8,128)(2,1)}, bf16[512,512]{1,0:T(8,128)(2,1)}, bf16[128,512]{1,0:T(8,128)(2,1)}, bf16...) custom-call(s32[16]{0:T(128)S(1)} %copy-done.21, ...), custom_call_target="tpu_custom_call" | custom-call | flops 8000000 | bytes 12000 | tf_op jit(solution)/shard_map/attend_kernel/pallas_call | solution.py:696
  150.2 9.3 %attend_kernel.2 = (bf16[512,512]{1,0:T(8,128)(2,1)}, bf16[512,512]{1,0:T(8,128)(2,1)}, bf16[512,512]{1,0:T(8,128)(2,1)}, bf16[128,512]{1,0:T(8,128)(2,1)}, bf16...) custom-call(s32[16]{0:T(128)S(1)} %copy-done.21, ...), custom_call_target="tpu_custom_call" | custom-call | flops 8000000 | bytes 12000 | tf_op jit(solution)/shard_map/attend_kernel/pallas_call | solution.py:696
  160.1 3.2 join_kernel.2.tok_ref
  163.2 5.5 %sens_kernel.1 = (f32[16,8,128]{2,1,0:T(8,128)S(1)}, f32[16,8,128]{2,1,0:T(8,128)S(1)}) custom-call(s32[1025]{0:T(1024)S(1)} %pad_add_fusion.seg_ref, f32[512,8,128]{2,1,0:T(8,128)S(1)} %bitcast.197, f32[16,8,128]{2,1,0:T(8,128)S(1)} %get-tuple-element.214.start_ref, f32[16,8,128]{2,1,0:T(8,128)S(1)} %get-tuple-element.354.rate_ref), custom_call_target="tpu_custom_call" | custom-call | flops 6000000 | bytes 1000 | tf_op jit(solution)/shard_map/sens_kernel/pallas_call | solution.py:1344
  168.8 3.2 join_kernel.3.cot_ref.g0.g1
  172.0 2.7 collective-permute-done.50.other_ref
  174.7 2.8 maximum_select_fusion.woo_ref
  181.6 14.8 %mlp_kernel.2 = (f32[512,1024]{1,0:T(8,128)}, bf16[512,1024]{1,0:T(8,128)(2,1)S(1)}, bf16[512,2048]{1,0:T(8,128)(2,1)}, bf16[512,2048]{1,0:T(8,128)(2,1)S(1)}, bf16[512,1024]{1,0:T(8,128)(2,1)}) custom-call(s32[16]{0:T(128)S(1)} %copy-done.21, bf16[512,512]{1,0:T(8,128)(2,1)} %get-tuple-element.212.own_ref.refs_11_, ...), custom_call_target="tpu_custom_call" | custom-call | flops 8000000 | bytes 24000 | tf_op jit(solution)/shard_map/mlp_kernel/pallas_call | solution.py:1060
  198.0 26.2 %mlp_kernel.3 = (f32[512,1024]{1,0:T(8,128)}, bf16[512,1024]{1,0:T(8,128)(2,1)S(1)}, bf16[512,2048]{1,0:T(8,128)(2,1)}, bf16[512,2048]{1,0:T(8,128)(2,1)S(1)}, bf16[512,1024]{1,0:T(8,128)(2,1)}) custom-call(s32[16]{0:T(128)S(1)} %copy-done.21, bf16[512,512]{1,0:T(8,128)(2,1)} %get-tuple-element.213.own_ref.refs_17_, ...), custom_call_target="tpu_custom_call" | custom-call | flops 8000000 | bytes 24000 | tf_op jit(solution)/shard_map/mlp_kernel/pallas_call | solution.py:1060
  225.8 13.2 %mlp_grad_kernel.1 = bf16[4,1024,1024]{2,1,0:T(8,128)(2,1)} custom-call(s32[16]{0:T(128)S(1)} %copy-done.21, bf16[512,1024]{1,0:T(8,128)(2,1)S(1)} %get-tuple-element.225.h0, bf16[512,1024]{1,0:T(8,128)(2,1)S(1)} %get-tuple-element.227.h1, bf16[1024,1024]{1,0:T(8,128)(2,1)S(1)} %copy-done, bf16[1024,1024]{1,0:T(8,128)(2,1)S(1)} %copy-done, ...), custom_call_target="tpu_custom_call" | custom-call | flops 8600000 | bytes 20000 | tf_op jit(solution)/shard_map/mlp_grad_kernel/pallas_call | solution.py:1124
  240.7 17.7 %attend_back_kernel.2 = (bf16[512,1024]{1,0:T(8,128)(2,1)}, f32[512,1024]{1,0:T(8,128)}, f32[1,1024]{1,0:T(1,128)S(1)}, bf16[512,512]{1,0:T(8,128)(2,1)}, bf16[5...) custom-call(s32[16]{0:T(128)S(1)} %copy-done.21, ...), custom_call_target="tpu_custom_call" | custom-call | flops 12000000 | bytes 20000 | tf_op jit(solution)/shard_map/attend_back_kernel/pallas_call | solution.py:871
  258.4 10.5 %mlp_out_kernel.1 = (bf16[1024,512]{1,0:T(8,128)(2,1)}, f32[1024,512]{1,0:T(8,128)}) custom-call(s32[16]{0:T(128)S(1)} %copy-done.21, bf16[512,2048]{1,0:T(8,128)(2,1)} %get-tuple-element.241.a0, bf16[512,2048]{1,0:T(8,128)(2,1)} %get-tuple-element.230.a1, bf16[4,1024,1024]{2,1,0:T(8,128)(2,1)} %bitcast.233, bf16[4,1024,1024]{2,1,0:T(8,128)(2,1)} %bitcast.234, ...), custom_call_target="tpu_custom_call" | custom-call | flops 4400000 | bytes 12000 | tf_op jit(solution)/shard_map/mlp_out_kernel/pallas_call | solution.py:1185
  269.9 16.8 %attend_back_kernel.3 = (bf16[512,1024]{1,0:T(8,128)(2,1)}, f32[512,1024]{1,0:T(8,128)}, f32[1,1024]{1,0:T(1,128)S(1)}, bf16[512,512]{1,0:T(8,128)(2,1)}, bf16[5...) custom-call(s32[16]{0:T(128)S(1)} %copy-done.21, ...), custom_call_target="tpu_custom_call" | custom-call | flops 12000000 | bytes 20000 | tf_op jit(solution)/shard_map/attend_back_kernel/pallas_call | solution.py:871
  286.7 1.8 collective-permute-start.59
  292.3 3.8 collective-permute-done.61
  296.4 1.9 back_total_kernel.1
  299.7 2.6 collective-permute-start.62
  303.2 9.8 %collective-permute-start.63 = (bf16[2,128,128]{2,1,0:T(8,128)(2,1)S(1)}, bf16[2,128,128]{2,1,0:T(8,128)(2,1)S(1)}, u32[]{:S(2)}, u32[]{:S(2)}) collective-permute-start(bf16[2,128,128]{2,1,0:T(8,128)(2,1)S(1)} %maximum_select_fusion.10), channel_id=1, source_target_pairs={{0,4},{2,6},{4,0},{6,2},{8,12},{10,14},{12,8},{14,10},{16,20},{18,... | collective-permute-start | bytes 196616 | tf_op jit(solution)/shard_map/ppermute | solution.py:103
  313.0 11.8 %attn_grad_kernel.1 = bf16[4,1024,512]{2,1,0:T(8,128)(2,1)} custom-call(s32[16]{0:T(128)S(1)} %copy-done.21, bf16[1024,1024]{1,0:T(8,128)(2,1)} %join_scaled_kernel.1.hid_ref.refs_0_.refs_1_, bf16[1024,1024]{1,0:T(8,128)(2,1)} %join_scaled_kernel.1.hid_ref.refs_0_.refs_1_, bf16[256,1024]{1,0:T(8,128)(2,1)} %bitcast.201, bf16[256,1024]{1,0:T(8,128)(2,1)} %bitcast.202, ...), custom_call_target="tpu_custom_call" | custom-call | flops 4600000 | bytes 14000 | tf_op jit(solution)/shard_map/attn_grad_kernel/pallas_call | solution.py:986
  325.4 3.2 dynamic-slice_bitcast_fusion
  335.7 1.7 collective-permute-start.65
  337.4 2.3 constant_dynamic-slice_fusion.3
  339.7 5.4 %collective-permute-done.65 = bf16[4,128,128]{2,1,0:T(8,128)(2,1)S(1)} collective-permute-done((bf16[4,128,128]{2,1,0:T(8,128)(2,1)S(1)}, bf16[4,128,128]{2,1,0:T(8,128)(2,1)S(1)}, u32[]{:S(2)}, u32[]{:S(2)}) %collective-permute-start.65) | collective-permute-done | bytes 131104 | tf_op jit(solution)/shard_map/ppermute | solution.py:103
  346.4 1.7 reduce.1
  351.6 3.4 sens_tail_kernel.1
  355.0 5.3 %collective-permute-done.66 = bf16[8,128,128]{2,1,0:T(8,128)(2,1)} collective-permute-done((bf16[8,128,128]{2,1,0:T(8,128)(2,1)}, bf16[8,128,128]{2,1,0:T(8,128)(2,1)}, u32[]{:S(2)}, u32[]{:S(2)}) %collective-permute-start.66) | collective-permute-done | bytes 262176 | tf_op jit(solution)/shard_map/ppermute | solution.py:103
  363.0 5.2 %back_scan_kernel.1 = (f32[512,8,128]{2,1,0:T(8,128)S(1)}, f32[16,8,128]{2,1,0:T(8,128)S(1)}) custom-call(s32[1025]{0:T(1024)S(1)} %pad_add_fusion.seg_ref, s32[16]{0:T(128)S(1)} %get-tuple-element.347.use_ref, bf16[16,128,128]{2,1,0:T(8,128)(2,1)S(1)} %maximum_select_fusion.2.all_ref, f32[128,8,128]{2,1,0:T(8,128)S(1)} %bitcast.205, ...), custom_call_target="tpu_custom_call" | custom-call | flops 4000000 | bytes 1000 | tf_op jit(solution)/shard_map/back_scan_kernel/pallas_call | solution.py:1471
  368.9 2.0 collective-permute-start.69
  370.9 2.2 fusion.9
  373.1 4.0 collective-permute-done.68
  377.2 2.1 fusion.25
  380.8 1.9 collective-permute-start.73
  382.7 4.1 collective-permute-done.70
  389.7 1.9 collective-permute-start.77
  391.6 3.3 fusion.16
  395.3 1.8 fusion.21
  397.1 2.4 collective-permute-start.72
  399.5 10.2 %collective-permute-start.74 = (bf16[256,512]{1,0:T(8,128)(2,1)S(1)}, bf16[256,512]{1,0:T(8,128)(2,1)S(1)}, u32[]{:S(2)}, u32[]{:S(2)}) collective-permute-start(bf16[256,512]{1,0:T(8,128)(2,1)S(1)} %get-tuple-element.327), channel_id=1, source_target_pairs={{8,0},{10,2},{16,8},{18,10},{24,16},{26,18},{28,24},{30,26},{20,28... | collective-permute-start | bytes 786440 | tf_op jit(solution)/shard_map/ppermute | solution.py:331
  409.7 3.2 collective-permute-done.76
  412.9 5.0 %collective-permute-done.77 = bf16[256,1024]{1,0:T(8,128)(2,1)S(1)} collective-permute-done((bf16[256,1024]{1,0:T(8,128)(2,1)}, bf16[256,1024]{1,0:T(8,128)(2,1)S(1)}, u32[]{:S(2)}, u32[]{:S(2)}) %collective-permute-start.77) | collective-permute-done | bytes 524320 | tf_op jit(solution)/shard_map/ppermute | solution.py:228
  418.0 3.3 collective-permute-start.78
  421.3 4.2 fusion.8
  427.9 2.2 collective-permute-done.79
  430.5 5.4 %fusion.50 = (bf16[1,256,2048]{2,1,0:T(8,128)(2,1)}, f32[1,256,2048]{2,1,0:T(8,128)}, f32[1,256,2048]{2,1,0:T(8,128)}, f32[1,256,2048]{2,1,0:T(8,128)}, f32[1,256,2048]{2,1,0:T(8,128)}) fusion(f32[1,256,2048]{2,1,0:T(8,128)S(1)} %copy-done.33, f32[]{:T(128)} %bitcast.78, f32[1,256,2048]{2,1,0:T(8,128)S(1)} %copy-done.43, f32[1,256,2048]{2,1,0:T(8,128)S(1)} %copy-done.44, ...), kind=kLoop, calls=%fused_computation.142 | loop fusion | flops 11010048 | bytes 16777220 | tf_op jit(solution)/shard_map/convert_element_type | solution.py:1570
  436.5 8.4 %conditional.6 = (bf16[256,512]{1,0:T(8,128)(2,1)}) conditional(s32[]{:T(128)} %bitcast.26, bf16[256,512]{1,0:T(8,128)(2,1)S(1)} %get-tuple-element.301, bf16[256,512]{1,0:T(8,128)(2,1)S(1)} %get-tuple-element.301, bf16[256,512]{1,0:T(8,128)(2,1)S(1)} %get-tuple-element.301, ...), branch_computations={%region_22.23_spmd, %region_23.24_spmd, %region_24.25_spmd, %regio... | conditional | bytes 1048624
  437.9 7.1 %collective-permute-done.18 = bf16[256,512]{1,0:T(8,128)(2,1)} collective-permute-done((bf16[256,512]{1,0:T(8,128)(2,1)S(1)}, bf16[256,512]{1,0:T(8,128)(2,1)}, u32[]{:S(2)}, u32[]{:S(2)}) %collective-permute-start.18) | collective-permute-done | bytes 262176 | tf_op jit(solution)/shard_map/cond/branch_0_fun/ppermute | solution.py:219
  446.7 3.9 fusion.52
  (313 shorter events, 85.5 us)
Async XLA Ops:
  7.2 19.2 %copy-start.2 = (bf16[1,1024,512]{2,1,0:T(8,128)(2,1)S(1)}, bf16[1,1024,512]{2,1,0:T(8,128)(2,1)}, u32[]{:S(2)}) copy-start(bf16[1,1024,512]{2,1,0:T(8,128)(2,1)} %param.54) | copy-start | bytes 3145732
  7.2 125.8 %all-gather.3.cloned.1.call-start = ((), (), s32[]{:S(2)}) async-start(), calls=%async_computation.1 | async-start | bytes 4456448 | tf_op jit(solution)/shard_map/all_gather | solution.py:1273
  10.6 17.6 %copy-start.60 = (s32[1,1024]{1,0:T(1,128)S(1)}, s32[1,1024]{1,0:T(1,128)}, u32[]{:S(2)}) copy-start(s32[1,1024]{1,0:T(1,128)} %param.56) | copy-start | bytes 12292
  10.6 20.0 %copy-start.50 = (f32[3,512,16]{1,2,0:T(8,128)S(1)}, f32[3,512,16]{1,2,0:T(8,128)}, u32[]{:S(2)}) copy-start(f32[3,512,16]{1,2,0:T(8,128)} %param.64) | copy-start | bytes 294916
  10.6 22.1 %copy-start.32 = (f32[1,256,2048]{2,1,0:T(8,128)S(1)}, f32[1,256,2048]{2,1,0:T(8,128)}, u32[]{:S(2)}) copy-start(f32[1,256,2048]{2,1,0:T(8,128)} %param.61) | copy-start | bytes 6291460
  14.2 10.5 %collective-permute-start = (bf16[256,512]{1,0:T(8,128)(2,1)S(1)}, bf16[256,512]{1,0:T(8,128)(2,1)}, u32[]{:S(2)}, u32[]{:S(2)}) collective-permute-start(bf16[256,512]{1,0:T(8,128)(2,1)S(1)} %param), channel_id=1, source_target_pairs={{0,8},{2,10},{4,12},{6,14},{1,9},{3,11},{5,13},{7,15}} | collective-permute-start | bytes 786440 | tf_op jit(solution)/shard_map/cond/branch_0_fun/ppermute | solution.py:219
  26.4 152.5 %all-gather.5.cloned.1.call-start = ((), (), s32[]{:S(2)}) async-start(), calls=%async_computation.2 | async-start | bytes 8912896 | tf_op jit(solution)/shard_map/all_gather | solution.py:1334
  26.7 11.4 %collective-permute-start.37 = (f32[1024]{0:T(1024)S(1)}, f32[1024]{0:T(1024)S(1)}, u32[]{:S(2)}, u32[]{:S(2)}) collective-permute-start(f32[1024]{0:T(1024)S(1)} %fusion.10), channel_id=1, source_target_pairs={{0,1},{1,0},{2,3},{3,2},{4,5},{5,4},{6,7},{7,6},{8,9},{9,8},{10,11... | collective-permute-start | bytes 12296 | tf_op jit(solution)/shard_map/ppermute | solution.py:83
  28.8 8.0 %collective-permute-start.39 = (s32[128]{0:T(128)S(1)}, s32[128]{0:T(128)S(1)}, u32[]{:S(2)}, u32[]{:S(2)}) collective-permute-start(s32[128]{0:T(128)S(1)} %get-tuple-element.342), channel_id=1, source_target_pairs={{0,2},{2,4},{4,6},{6,8},{8,10},{10,12},{12,14},{14,16},{16,18},{18... | collective-permute-start | bytes 1544 | tf_op jit(solution)/shard_map/ppermute | solution.py:1278
  30.0 28.4 %collective-permute-start.36 = (bf16[1024,512]{1,0:T(8,128)(2,1)S(1)}, bf16[1024,512]{1,0:T(8,128)(2,1)}, u32[]{:S(2)}, u32[]{:S(2)}) collective-permute-start(bf16[1024,512]{1,0:T(8,128)(2,1)S(1)} %bitcast.193), channel_id=1, source_target_pairs={{0,1},{1,0},{2,3},{3,2},{4,5},{5,4},{6,7},{7,6},{8,9},{9,8},{10,11... | collective-permute-start | bytes 3145736 | tf_op jit(solution)/shard_map/ppermute | solution.py:83
  38.1 27.7 %collective-permute-start.40 = (bf16[256,1024]{1,0:T(8,128)(2,1)}, bf16[256,1024]{1,0:T(8,128)(2,1)}, u32[]{:S(2)}, u32[]{:S(2)}) collective-permute-start(bf16[256,1024]{1,0:T(8,128)(2,1)} %slice.180), channel_id=1, source_target_pairs={{0,8},{2,10},{4,12},{6,14},{8,0},{10,2},{12,4},{14,6},{16,24},{18,... | collective-permute-start | bytes 1572872 | tf_op jit(solution)/shard_map/ppermute | solution.py:228
  41.4 39.0 %collective-permute-start.41 = (bf16[256,1024]{1,0:T(8,128)(2,1)}, bf16[256,1024]{1,0:T(8,128)(2,1)}, u32[]{:S(2)}, u32[]{:S(2)}) collective-permute-start(bf16[256,1024]{1,0:T(8,128)(2,1)} %slice.180), channel_id=1, source_target_pairs={{0,16},{2,18},{4,20},{6,22},{8,24},{10,26},{12,28},{14,30},{16,0},... | collective-permute-start | bytes 1572872 | tf_op jit(solution)/shard_map/ppermute | solution.py:228
  41.4 43.9 %copy-start.56 = (f32[1024]{0:T(1024)}, f32[1024]{0:T(1024)S(1)}, u32[]{:S(2)}) copy-start(f32[1024]{0:T(1024)S(1)} %add_rsqrt_fusion) | copy-start | bytes 12292
  45.2 118.1 %copy-start.3 = (f32[2,512,4,128]{3,2,0,1:T(4,128)}, f32[2,512,4,128]{3,2,0,1:T(4,128)S(1)}, u32[]{:S(2)}) copy-start(f32[2,512,4,128]{3,2,0,1:T(4,128)S(1)} %fusion.17) | copy-start | bytes 6291460
  50.7 1.9 collective-permute-start.42
  52.7 4.7 %collective-permute-start.43 = (bf16[2,144,128]{2,1,0:T(8,128)(2,1)S(1)}, bf16[2,144,128]{2,1,0:T(8,128)(2,1)}, u32[]{:S(2)}, u32[]{:S(2)}) collective-permute-start(bf16[2,144,128]{2,1,0:T(8,128)(2,1)S(1)} %maximum_select_fusion.9), channel_id=1, source_target_pairs={{0,4},{2,6},{4,0},{6,2},{8,12},{10,14},{12,8},{14,10},{16,20},{18,... | collective-permute-start | bytes 221192 | tf_op jit(solution)/shard_map/ppermute | solution.py:103
  53.5 28.8 %copy-start.38 = (bf16[256,2048]{1,0:T(8,128)(2,1)S(1)}, bf16[256,2048]{1,0:T(8,128)(2,1)}, u32[]{:S(2)}) copy-start(bf16[256,2048]{1,0:T(8,128)(2,1)} %convert_bitcast_fusion) | copy-start | bytes 3145732
  58.4 23.1 %collective-permute-start.44 = (bf16[4,144,128]{2,1,0:T(8,128)(2,1)S(1)}, bf16[4,144,128]{2,1,0:T(8,128)(2,1)S(1)}, u32[]{:S(2)}, u32[]{:S(2)}) collective-permute-start(bf16[4,144,128]{2,1,0:T(8,128)(2,1)S(1)} %maximum_select_fusion.7), channel_id=1, source_target_pairs={{0,8},{2,10},{4,12},{6,14},{8,0},{10,2},{12,4},{14,6},{16,24},{18,... | collective-permute-start | bytes 442376 | tf_op jit(solution)/shard_map/ppermute | solution.py:103
  80.4 29.0 %copy-start.21 = (s32[16]{0:T(128)S(1)}, s32[16]{0:T(128)}, u32[]{:S(2)}) copy-start(s32[16]{0:T(128)} %get-tuple-element.202.host_ref) | copy-start | bytes 196
  83.2 305.4 %reduce-scatter.2.cloned.1.call-start = ((), (), s32[]{:S(2)}) async-start(), calls=%async_computation.3 | async-start | bytes 8912896 | tf_op jit(solution)/shard_map/reduce_scatter | solution.py:1412
  83.2 32.0 %collective-permute-start.46 = (bf16[1024,512]{1,0:T(8,128)(2,1)}, bf16[1024,512]{1,0:T(8,128)(2,1)}, u32[]{:S(2)}, u32[]{:S(2)}) collective-permute-start(bf16[1024,512]{1,0:T(8,128)(2,1)} %bitcast.207), channel_id=1, source_target_pairs={{0,1},{1,0},{2,3},{3,2},{4,5},{5,4},{6,7},{7,6},{8,9},{9,8},{10,11... | collective-permute-start | bytes 3145736 | tf_op jit(solution)/shard_map/ppermute | solution.py:83
  84.6 29.5 %collective-permute-start.45 = (bf16[8,144,128]{2,1,0:T(8,128)(2,1)}, bf16[8,144,128]{2,1,0:T(8,128)(2,1)}, u32[]{:S(2)}, u32[]{:S(2)}) collective-permute-start(bf16[8,144,128]{2,1,0:T(8,128)(2,1)} %maximum_select_fusion.3), channel_id=1, source_target_pairs={{0,16},{2,18},{4,20},{6,22},{8,24},{10,26},{12,28},{14,30},{16,0},... | collective-permute-start | bytes 884744 | tf_op jit(solution)/shard_map/ppermute | solution.py:103
  84.6 24.9 %collective-permute-start.38 = (f32[2,512]{1,0:T(2,128)S(1)}, f32[2,512]{1,0:T(2,128)S(1)}, u32[]{:S(2)}, u32[]{:S(2)}) collective-permute-start(f32[2,512]{1,0:T(2,128)S(1)} %copy-done.63), channel_id=1, source_target_pairs={{0,1},{1,0},{2,3},{3,2},{4,5},{5,4},{6,7},{7,6},{8,9},{9,8},{10,11... | collective-permute-start | bytes 12296 | tf_op jit(solution)/shard_map/ppermute | solution.py:83
  119.6 16.8 %copy-start.74 = (s32[128]{0:T(128)S(1)}, s32[128]{0:T(128)}, u32[]{:S(2)}) copy-start(s32[128]{0:T(128)} %copy-done.73) | copy-start | bytes 1540
  123.8 11.1 %collective-permute-start.49 = (bf16[1,128,512]{2,1,0:T(8,128)(2,1)}, bf16[1,128,512]{2,1,0:T(8,128)(2,1)}, u32[]{:S(2)}, u32[]{:S(2)}) collective-permute-start(bf16[1,128,512]{2,1,0:T(8,128)(2,1)} %slice.153), channel_id=1, source_target_pairs={{0,1},{1,0},{2,3},{3,2},{4,5},{5,4},{6,7},{7,6},{8,9},{9,8},{10,11... | collective-permute-start | bytes 393224 | tf_op jit(solution)/shard_map/ppermute | solution.py:83
  128.0 8.5 %collective-permute-start.47 = (bf16[128,512]{1,0:T(8,128)(2,1)}, bf16[128,512]{1,0:T(8,128)(2,1)}, u32[]{:S(2)}, u32[]{:S(2)}) collective-permute-start(bf16[128,512]{1,0:T(8,128)(2,1)} %bitcast.189), channel_id=1, source_target_pairs={{0,2},{1,3},{2,4},{3,5},{4,6},{5,7},{6,8},{7,9},{8,10},{9,11},{10,... | collective-permute-start | bytes 393224 | tf_op jit(solution)/shard_map/ppermute | solution.py:345
  129.9 6.5 %collective-permute-start.48 = (bf16[128,512]{1,0:T(8,128)(2,1)}, bf16[128,512]{1,0:T(8,128)(2,1)}, u32[]{:S(2)}, u32[]{:S(2)}) collective-permute-start(bf16[128,512]{1,0:T(8,128)(2,1)} %bitcast.189), channel_id=1, source_target_pairs={{0,3},{1,2},{2,5},{3,4},{4,7},{5,6},{6,9},{7,8},{8,11},{9,10},{10,... | collective-permute-start | bytes 393224 | tf_op jit(solution)/shard_map/ppermute | solution.py:345
  135.0 24.9 %collective-permute-start.52 = (bf16[512,512]{1,0:T(8,128)(2,1)}, bf16[512,512]{1,0:T(8,128)(2,1)}, u32[]{:S(2)}, u32[]{:S(2)}) collective-permute-start(bf16[512,512]{1,0:T(8,128)(2,1)} %dynamic-slice_bitcast_fusion.1), channel_id=1, source_target_pairs={{0,1},{1,0},{2,3},{3,2},{4,5},{5,4},{6,7},{7,6},{8,9},{9,8},{10,11... | collective-permute-start | bytes 1572872 | tf_op jit(solution)/shard_map/ppermute | solution.py:83
  148.6 23.4 %collective-permute-start.51 = (bf16[512,512]{1,0:T(8,128)(2,1)}, bf16[512,512]{1,0:T(8,128)(2,1)}, u32[]{:S(2)}, u32[]{:S(2)}) collective-permute-start(bf16[512,512]{1,0:T(8,128)(2,1)} %get-tuple-element.213.own_ref.refs_17_), channel_id=1, source_target_pairs={{0,1},{1,0},{2,3},{3,2},{4,5},{5,4},{6,7},{7,6},{8,9},{9,8},{10,11... | collective-permute-start | bytes 1572872 | tf_op jit(solution)/shard_map/ppermute | solution.py:83
  159.5 15.2 %collective-permute-start.50 = (bf16[512,512]{1,0:T(8,128)(2,1)}, bf16[512,512]{1,0:T(8,128)(2,1)}, u32[]{:S(2)}, u32[]{:S(2)}) collective-permute-start(bf16[512,512]{1,0:T(8,128)(2,1)} %get-tuple-element.212.own_ref.refs_11_), channel_id=1, source_target_pairs={{0,1},{1,0},{2,3},{3,2},{4,5},{5,4},{6,7},{7,6},{8,9},{9,8},{10,11... | collective-permute-start | bytes 1572872 | tf_op jit(solution)/shard_map/ppermute | solution.py:83
  159.9 14.8 %collective-permute-start.53 = (bf16[512,512]{1,0:T(8,128)(2,1)}, bf16[512,512]{1,0:T(8,128)(2,1)}, u32[]{:S(2)}, u32[]{:S(2)}) collective-permute-start(bf16[512,512]{1,0:T(8,128)(2,1)} %collective-permute-done.52), channel_id=1, source_target_pairs={{0,2},{2,0},{4,6},{6,4},{8,10},{10,8},{12,14},{14,12},{16,18},{18,... | collective-permute-start | bytes 1572872 | tf_op jit(solution)/shard_map/ppermute | solution.py:1378
  196.4 27.8 %copy-start.11 = (bf16[512,2048]{1,0:T(8,128)(2,1)S(1)}, bf16[512,2048]{1,0:T(8,128)(2,1)}, u32[]{:S(2)}) copy-start(bf16[512,2048]{1,0:T(8,128)(2,1)} %get-tuple-element.241.a0) | copy-start | bytes 6291460
  196.4 42.5 %collective-permute-start.54 = (bf16[512,1024]{1,0:T(8,128)(2,1)}, bf16[512,1024]{1,0:T(8,128)(2,1)}, u32[]{:S(2)}, u32[]{:S(2)}) collective-permute-start(bf16[512,1024]{1,0:T(8,128)(2,1)} %get-tuple-element.224.own_ref), channel_id=1, source_target_pairs={{0,1},{1,0},{2,3},{3,2},{4,5},{5,4},{6,7},{7,6},{8,9},{9,8},{10,11... | collective-permute-start | bytes 3145736 | tf_op jit(solution)/shard_map/ppermute | solution.py:83
  240.2 28.8 %collective-permute-start.56 = (bf16[512,1024]{1,0:T(8,128)(2,1)S(1)}, bf16[512,1024]{1,0:T(8,128)(2,1)S(1)}, u32[]{:S(2)}, u32[]{:S(2)}) collective-permute-start(bf16[512,1024]{1,0:T(8,128)(2,1)S(1)} %copy-done.48), channel_id=1, source_target_pairs={{0,1},{1,0},{2,3},{3,2},{4,5},{5,4},{6,7},{7,6},{8,9},{9,8},{10,11... | collective-permute-start | bytes 3145736 | tf_op jit(solution)/shard_map/ppermute | solution.py:83
  286.7 5.4 %collective-permute-start.59 = (bf16[128,512]{1,0:T(8,128)(2,1)S(1)}, bf16[128,512]{1,0:T(8,128)(2,1)S(1)}, u32[]{:S(2)}, u32[]{:S(2)}) collective-permute-start(bf16[128,512]{1,0:T(8,128)(2,1)S(1)} %get-tuple-element.262), channel_id=1, source_target_pairs={{0,1},{1,0},{2,3},{3,2},{4,5},{5,4},{6,7},{7,6},{8,9},{9,8},{10,11... | collective-permute-start | bytes 393224 | tf_op jit(solution)/shard_map/ppermute | solution.py:83
  288.5 3.8 collective-permute-start.60
  289.8 6.3 %collective-permute-start.61 = (bf16[128,512]{1,0:T(8,128)(2,1)S(1)}, bf16[128,512]{1,0:T(8,128)(2,1)S(1)}, u32[]{:S(2)}, u32[]{:S(2)}) collective-permute-start(bf16[128,512]{1,0:T(8,128)(2,1)S(1)} %get-tuple-element.264), channel_id=1, source_target_pairs={{2,1},{3,0},{4,3},{5,2},{6,5},{7,4},{8,7},{9,6},{10,9},{11,8},{12,... | collective-permute-start | bytes 393224 | tf_op jit(solution)/shard_map/ppermute | solution.py:345
  299.7 3.4 collective-permute-start.62
  303.2 21.6 %collective-permute-start.63 = (bf16[2,128,128]{2,1,0:T(8,128)(2,1)S(1)}, bf16[2,128,128]{2,1,0:T(8,128)(2,1)S(1)}, u32[]{:S(2)}, u32[]{:S(2)}) collective-permute-start(bf16[2,128,128]{2,1,0:T(8,128)(2,1)S(1)} %maximum_select_fusion.10), channel_id=1, source_target_pairs={{0,4},{2,6},{4,0},{6,2},{8,12},{10,14},{12,8},{14,10},{16,20},{18,... | collective-permute-start | bytes 196616 | tf_op jit(solution)/shard_map/ppermute | solution.py:103
  328.6 33.0 %collective-permute-start.64 = (bf16[8,256,512]{2,1,0:T(8,128)(2,1)}, bf16[8,256,512]{2,1,0:T(8,128)(2,1)}, u32[]{:S(2)}, u32[]{:S(2)}) collective-permute-start(bf16[8,256,512]{2,1,0:T(8,128)(2,1)} %dynamic-slice_bitcast_fusion), channel_id=1, source_target_pairs={{0,2},{2,0},{4,6},{6,4},{8,10},{10,8},{12,14},{14,12},{16,18},{18,... | collective-permute-start | bytes 6291464 | tf_op jit(solution)/shard_map/ppermute | solution.py:315
  331.9 39.0 %collective-permute-start.58 = (bf16[512,512]{1,0:T(8,128)(2,1)}, bf16[512,512]{1,0:T(8,128)(2,1)}, u32[]{:S(2)}, u32[]{:S(2)}) collective-permute-start(bf16[512,512]{1,0:T(8,128)(2,1)} %get-tuple-element.260), channel_id=1, source_target_pairs={{0,1},{1,0},{2,3},{3,2},{4,5},{5,4},{6,7},{7,6},{8,9},{9,8},{10,11... | collective-permute-start | bytes 1572872 | tf_op jit(solution)/shard_map/ppermute | solution.py:83
  332.6 38.3 %collective-permute-start.57 = (bf16[512,512]{1,0:T(8,128)(2,1)}, bf16[512,512]{1,0:T(8,128)(2,1)}, u32[]{:S(2)}, u32[]{:S(2)}) collective-permute-start(bf16[512,512]{1,0:T(8,128)(2,1)} %get-tuple-element.259), channel_id=1, source_target_pairs={{0,1},{1,0},{2,3},{3,2},{4,5},{5,4},{6,7},{7,6},{8,9},{9,8},{10,11... | collective-permute-start | bytes 1572872 | tf_op jit(solution)/shard_map/ppermute | solution.py:83
  334.0 55.7 %collective-permute-start.55 = (bf16[1024,512]{1,0:T(8,128)(2,1)}, bf16[1024,512]{1,0:T(8,128)(2,1)}, u32[]{:S(2)}, u32[]{:S(2)}) collective-permute-start(bf16[1024,512]{1,0:T(8,128)(2,1)} %get-tuple-element.244), channel_id=1, source_target_pairs={{0,1},{1,0},{2,3},{3,2},{4,5},{5,4},{6,7},{7,6},{8,9},{9,8},{10,11... | collective-permute-start | bytes 3145736 | tf_op jit(solution)/shard_map/ppermute | solution.py:83
  335.7 9.4 %collective-permute-start.65 = (bf16[4,128,128]{2,1,0:T(8,128)(2,1)S(1)}, bf16[4,128,128]{2,1,0:T(8,128)(2,1)S(1)}, u32[]{:S(2)}, u32[]{:S(2)}) collective-permute-start(bf16[4,128,128]{2,1,0:T(8,128)(2,1)S(1)} %copy-done.54), channel_id=1, source_target_pairs={{0,8},{2,10},{4,12},{6,14},{8,0},{10,2},{12,4},{14,6},{16,24},{18,... | collective-permute-start | bytes 393224 | tf_op jit(solution)/shard_map/ppermute | solution.py:103
  345.8 14.4 %collective-permute-start.66 = (bf16[8,128,128]{2,1,0:T(8,128)(2,1)}, bf16[8,128,128]{2,1,0:T(8,128)(2,1)}, u32[]{:S(2)}, u32[]{:S(2)}) collective-permute-start(bf16[8,128,128]{2,1,0:T(8,128)(2,1)} %maximum_select_fusion.6), channel_id=1, source_target_pairs={{0,16},{2,18},{4,20},{6,22},{8,24},{10,26},{12,28},{14,30},{16,0},... | collective-permute-start | bytes 786440 | tf_op jit(solution)/shard_map/ppermute | solution.py:103
  368.8 8.3 %collective-permute-start.68 = (bf16[256,512]{1,0:T(8,128)(2,1)S(1)}, bf16[256,512]{1,0:T(8,128)(2,1)S(1)}, u32[]{:S(2)}, u32[]{:S(2)}) collective-permute-start(bf16[256,512]{1,0:T(8,128)(2,1)S(1)} %get-tuple-element.289), channel_id=1, source_target_pairs={{0,8},{2,10},{8,16},{10,18},{16,24},{18,26},{24,28},{26,30},{28,20... | collective-permute-start | bytes 786440 | tf_op jit(solution)/shard_map/ppermute | solution.py:327
  368.9 8.3 %collective-permute-start.69 = (bf16[256,512]{1,0:T(8,128)(2,1)S(1)}, bf16[256,512]{1,0:T(8,128)(2,1)S(1)}, u32[]{:S(2)}, u32[]{:S(2)}) collective-permute-start(bf16[256,512]{1,0:T(8,128)(2,1)S(1)} %get-tuple-element.290), channel_id=1, source_target_pairs={{8,0},{10,2},{16,8},{18,10},{24,16},{26,18},{28,24},{30,26},{20,28... | collective-permute-start | bytes 786440 | tf_op jit(solution)/shard_map/ppermute | solution.py:331
  379.3 7.5 %collective-permute-start.70 = (bf16[256,512]{1,0:T(8,128)(2,1)S(1)}, bf16[256,512]{1,0:T(8,128)(2,1)S(1)}, u32[]{:S(2)}, u32[]{:S(2)}) collective-permute-start(bf16[256,512]{1,0:T(8,128)(2,1)S(1)} %get-tuple-element.291), channel_id=1, source_target_pairs={{0,8},{2,10},{8,16},{10,18},{16,24},{18,26},{24,28},{26,30},{28,20... | collective-permute-start | bytes 786440 | tf_op jit(solution)/shard_map/ppermute | solution.py:327
  379.8 15.0 %collective-permute-start.67 = (f32[1024]{0:T(1024)S(1)}, f32[1024]{0:T(1024)S(1)}, u32[]{:S(2)}, u32[]{:S(2)}) collective-permute-start(f32[1024]{0:T(1024)S(1)} %fusion.43), channel_id=1, source_target_pairs={{0,1},{1,0},{2,3},{3,2},{4,5},{5,4},{6,7},{7,6},{8,9},{9,8},{10,11... | collective-permute-start | bytes 12296 | tf_op jit(solution)/shard_map/ppermute | solution.py:83
  380.8 14.1 %collective-permute-start.73 = (bf16[256,512]{1,0:T(8,128)(2,1)}, bf16[256,512]{1,0:T(8,128)(2,1)}, u32[]{:S(2)}, u32[]{:S(2)}) collective-permute-start(bf16[256,512]{1,0:T(8,128)(2,1)} %get-tuple-element.292), channel_id=1, source_target_pairs={{8,0},{10,2},{16,8},{18,10},{24,16},{26,18},{28,24},{30,26},{20,28... | collective-permute-start | bytes 786440 | tf_op jit(solution)/shard_map/ppermute | solution.py:331
  388.0 7.4 %collective-permute-start.71 = (bf16[256,512]{1,0:T(8,128)(2,1)S(1)}, bf16[256,512]{1,0:T(8,128)(2,1)}, u32[]{:S(2)}, u32[]{:S(2)}) collective-permute-start(bf16[256,512]{1,0:T(8,128)(2,1)S(1)} %fusion.23), channel_id=1, source_target_pairs={{0,8},{2,10},{8,16},{10,18},{16,24},{18,26},{24,28},{26,30},{28,20... | collective-permute-start | bytes 786440 | tf_op jit(solution)/shard_map/ppermute | solution.py:327
  388.6 24.3 %collective-permute-start.76 = (bf16[256,1024]{1,0:T(8,128)(2,1)}, bf16[256,1024]{1,0:T(8,128)(2,1)S(1)}, u32[]{:S(2)}, u32[]{:S(2)}) collective-permute-start(bf16[256,1024]{1,0:T(8,128)(2,1)} %reduce-scatter.2.cloned.1.call-done), channel_id=1, source_target_pairs={{0,8},{2,10},{4,12},{6,14},{8,0},{10,2},{12,4},{14,6},{16,24},{18,... | collective-permute-start | bytes 1572872 | tf_op jit(solution)/shard_map/ppermute | solution.py:228
  389.7 28.3 %collective-permute-start.77 = (bf16[256,1024]{1,0:T(8,128)(2,1)}, bf16[256,1024]{1,0:T(8,128)(2,1)S(1)}, u32[]{:S(2)}, u32[]{:S(2)}) collective-permute-start(bf16[256,1024]{1,0:T(8,128)(2,1)} %reduce-scatter.2.cloned.1.call-done), channel_id=1, source_target_pairs={{0,16},{2,18},{4,20},{6,22},{8,24},{10,26},{12,28},{14,30},{16,0},... | collective-permute-start | bytes 1572872 | tf_op jit(solution)/shard_map/ppermute | solution.py:228
  391.6 29.7 %copy-start.42 = (f32[512,512]{1,0:T(8,128)S(1)}, f32[512,512]{1,0:T(8,128)}, u32[]{:S(2)}) copy-start(f32[512,512]{1,0:T(8,128)} %get-tuple-element.258) | copy-start | bytes 3145732
  394.8 26.5 %copy-start.34 = (f32[512,512]{1,0:T(8,128)S(1)}, f32[512,512]{1,0:T(8,128)}, u32[]{:S(2)}) copy-start(f32[512,512]{1,0:T(8,128)} %constant_dynamic-slice_fusion.2) | copy-start | bytes 3145732
  394.8 26.5 %copy-start.35 = (f32[512,512]{1,0:T(8,128)S(1)}, f32[512,512]{1,0:T(8,128)}, u32[]{:S(2)}) copy-start(f32[512,512]{1,0:T(8,128)} %constant_dynamic-slice_fusion.3) | copy-start | bytes 3145732
  394.8 26.5 %copy-start.40 = (f32[512,512]{1,0:T(8,128)S(1)}, f32[512,512]{1,0:T(8,128)}, u32[]{:S(2)}) copy-start(f32[512,512]{1,0:T(8,128)} %get-tuple-element.257) | copy-start | bytes 3145732
  394.8 14.9 %collective-permute-start.75 = (f32[34,512]{1,0:T(8,128)S(1)}, f32[34,512]{1,0:T(8,128)S(1)}, u32[]{:S(2)}, u32[]{:S(2)}) collective-permute-start(f32[34,512]{1,0:T(8,128)S(1)} %pad_maximum_fusion.3), channel_id=1, source_target_pairs={{0,2},{2,0},{4,6},{6,4},{8,10},{10,8},{12,14},{14,12},{16,18},{18,... | collective-permute-start | bytes 208904 | tf_op jit(solution)/shard_map/ppermute | solution.py:117
  397.1 29.6 %collective-permute-start.72 = (bf16[256,512]{1,0:T(8,128)(2,1)S(1)}, bf16[256,512]{1,0:T(8,128)(2,1)S(1)}, u32[]{:S(2)}, u32[]{:S(2)}) collective-permute-start(bf16[256,512]{1,0:T(8,128)(2,1)S(1)} %get-tuple-element.326), channel_id=1, source_target_pairs={{0,8},{2,10},{8,16},{10,18},{16,24},{18,26},{24,28},{26,30},{28,20... | collective-permute-start | bytes 786440 | tf_op jit(solution)/shard_map/ppermute | solution.py:327
  399.5 27.2 %collective-permute-start.74 = (bf16[256,512]{1,0:T(8,128)(2,1)S(1)}, bf16[256,512]{1,0:T(8,128)(2,1)S(1)}, u32[]{:S(2)}, u32[]{:S(2)}) collective-permute-start(bf16[256,512]{1,0:T(8,128)(2,1)S(1)} %get-tuple-element.327), channel_id=1, source_target_pairs={{8,0},{10,2},{16,8},{18,10},{24,16},{26,18},{28,24},{30,26},{20,28... | collective-permute-start | bytes 786440 | tf_op jit(solution)/shard_map/ppermute | solution.py:331
  418.0 7.5 %collective-permute-start.78 = (f32[34,512]{1,0:T(8,128)S(1)}, f32[34,512]{1,0:T(8,128)S(1)}, u32[]{:S(2)}, u32[]{:S(2)}) collective-permute-start(f32[34,512]{1,0:T(8,128)S(1)} %add.414), channel_id=1, source_target_pairs={{0,4},{2,6},{4,0},{6,2},{8,12},{10,14},{12,8},{14,10},{16,20},{18,... | collective-permute-start | bytes 208904 | tf_op jit(solution)/shard_map/ppermute | solution.py:117
  425.5 4.5 collective-permute-start.79
  430.1 6.4 %collective-permute-start.80 = (f32[34,512]{1,0:T(8,128)S(1)}, f32[34,512]{1,0:T(8,128)S(1)}, u32[]{:S(2)}, u32[]{:S(2)}) collective-permute-start(f32[34,512]{1,0:T(8,128)S(1)} %add.416), channel_id=1, source_target_pairs={{0,16},{2,18},{4,20},{6,22},{8,24},{10,26},{12,28},{14,30},{16,0},... | collective-permute-start | bytes 208904 | tf_op jit(solution)/shard_map/ppermute | solution.py:117
  436.6 8.4 %collective-permute-start.18 = (bf16[256,512]{1,0:T(8,128)(2,1)S(1)}, bf16[256,512]{1,0:T(8,128)(2,1)}, u32[]{:S(2)}, u32[]{:S(2)}) collective-permute-start(bf16[256,512]{1,0:T(8,128)(2,1)S(1)} %param.18), channel_id=1, source_target_pairs={{8,0},{10,2},{12,4},{14,6},{9,1},{11,3},{13,5},{15,7}} | collective-permute-start | bytes 786440 | tf_op jit(solution)/shard_map/cond/branch_0_fun/ppermute | solution.py:219
  (62 other events, 373.2 us)
Sparse Core Ops, SparseCore 0:
  26.5 73.5 all-gather.2
  102.8 75.9 all-gather.4
  239.1 106.5 reduce-scatter.1
where the time goes:
time: 466 us; the launch traced here: 458 us
  Pallas kernels  163 us (35%)
  waiting for transfers between devices  99.9 us (21%)
  starting transfers between devices  76.3 us (16%)
  other arithmetic  57.3 us (12%)
  local copies, waits for them, and re-layouts  38.6 us (8%)
  between operations  23.1 us (5%)
    pallas_call x2, Pallas kernels, mlp_block(): call(mlp_kernel, (2 * per,), [whole((BL, half_width)), whole((BL, half_wi...  41 us
    pallas_call x2, Pallas kernels, attend_backward(): call(attend_back_kernel, (pairs + 2,), [whole((BL, D)), whole((BL, D)), p...  34.4 us
    ppermute x4, waiting for transfers between devices, across(): lax.ppermute(values, 'dp', [(g * size + j, (g ^ bit) * size + j) for g in...  29.7 us
    ppermute x15, waiting for transfers between devices, swap_x(): return lax.ppermute(values, 'tensor', SWAP)  26.8 us
    pallas_call x2, Pallas kernels, attend_forward(): call(attend_kernel, (pairs,), [pl.BlockSpec((BL, D), lambda p, s: (block,...  18.7 us
    unnamed x156, local copies, waits for them, and re-layouts  18.3 us
    ppermute x8, starting transfers between devices, gather_round(): other = lax.ppermute(held, 'dp', [(i, i ^ step) for i in range(count)])  16.6 us
    ppermute x8, waiting for transfers between devices, gather_round(): other = lax.ppermute(held, 'dp', [(i, i ^ step) for i in range(count)])  14.9 us
  transfers between devices with their start and end apart: 50, of which 22 were waited for; matrix products, arithmetic and copies ran while one was open for 15% of the time, Pallas kernels for 32%

commit v1 on v0

--- a/solution.py
+++ b/solution.py
@@ -1451,7 +1451,9 @@
             + shift_tails(ctx_sent[0], -1, True).astype(f32)
         ]
     )
-    tail_grad_lanes = to_lanes(grad_tails.reshape(blocks * CTX, width), blocks, CTX)
+    tail_grad_lanes = gate(
+        to_lanes(grad_tails.reshape(blocks * CTX, width), blocks, CTX), out_received
+    )
     own_back, device_back = plain(back_total_kernel, 1, 3, [state_shape, state_shape], 10**9)(
         seg_ext, tail_grad_lanes, rate_lanes, reading_lanes
     )
@@ -1459,12 +1461,16 @@
     lows[0] = gate(lows[0], back_all)
     attn_sum_in = attn_grads(hosts, hidden_full, context_full, lows, grad_blocks, width)
     received = [swap_x(v) for v in parts_sent]
-    for k in range(1, gather_rounds()):
+    for k in range(1, gather_rounds() - 1):
         if k == 2:
             back_all, attn_sum_in = together(back_all, attn_sum_in)
         back_all = gather_round(back_all, k)
     part, up, down = ring.start(attn_sum_in.reshape(dp_count, -1, width))
     up, down, back_all = together(up, down, back_all)
+    back_all = gather_round(back_all, gather_rounds() - 1)
+    up, down = ring.step(0, part, up, down)
+    up, down, back_all, mlp_sum = together(up, down, back_all, mlp_sum)
+    mlp_back = exchange_groups(mlp_sum, near)
     grad_c_lanes, grad_a_lanes, sens_end = plain(
         sens_tail_kernel, 1, 5, [state_shape] * 3, 2 * 10**9
     )(seg_ext, hidden_lanes, tail_grad_lanes, sens_states, sens_starts, rate_lanes)
@@ -1486,9 +1492,7 @@
         rate_lanes,
         reading_lanes,
     )
-    for k in range(ring.far_up):
-        if k == 1:
-            up, down = together(up, down, grad_lanes)[:2]
+    for k in range(1, ring.far_up):
         up, down = ring.step(k, part, up, down)
     attn_sum = (part(0) + up.astype(f32) + down.astype(f32)).astype(bf16)
     grad_channels = lax.optimization_barrier(
@@ -1502,7 +1506,7 @@
     )
     row_other = swap_x(row_here)
     row_total = row_here + row_other
-    block_out = (out_own + out_received.astype(f32)).astype(bf16)
+    block_out = (out_own + gate(out_received, row_other).astype(f32)).astype(bf16)
     grad_hidden = part_own + received.astype(f32) + grad_channels
     grad_tokens = jnp.concatenate(grad_mids, axis=0) + inverse_one[:, None] * (
         grad_hidden * norm_gains[0] - scaled_own * (row_total / D)[:, None]
@@ -1516,8 +1520,6 @@
     small = jnp.concatenate(
         [merged(grad_c_lanes), merged(grad_a_lanes), gain_one[None], gain_two_sum[None]], axis=0
     )
-    small, mlp_sum = together(small, mlp_sum)
-    mlp_back = exchange_groups(mlp_sum, near)
     small, mlp_back = total_dp(small, mlp_back)
     grad_c, grad_a = small[:STATE], small[STATE : 2 * STATE]
     gains_grad = small[2 * STATE :]

time: 466 us -> 456 us (0.979)
  waiting for transfers between devices: 99.9 us -> 94.3 us
    ppermute x4, waiting for transfers between devices: 29.7 us -> 9.18 us  [across(): lax.ppermute(values, 'dp', [(g * size + j, (g ^ bit) * size + j) for g in...]
    ppermute x3, starting transfers between devices: 14 us -> 0.98 us  [step(): down = lax.ppermute(down, 'dp', self.down)]
    ppermute x8, waiting for transfers between devices: 14.9 us -> 23.1 us  [gather_round(): other = lax.ppermute(held, 'dp', [(i, i ^ step) for i in range(count)])]
    ppermute x4, waiting for transfers between devices: 2.72 us -> 7.74 us  [total_dp(): lax.ppermute(values, 'dp', [(i, i ^ 1 << k) for i in range(count)])]
    unnamed x156 -> x168, local copies, waits for them, and re-layouts: 18.3 us -> 18.4 us
  transfers between devices with their start and end apart: 50 -> 50, of which waited for: 22 -> 20; matrix products, arithmetic and copies ran while one was open for 15% -> 15% of each run, Pallas kernels for 32% -> 32%
where the time goes in v1:
time: 456 us; the launch traced here: 453 us
  Pallas kernels  163 us (36%)
  waiting for transfers between devices  94.3 us (21%)
  starting transfers between devices  75.7 us (17%)
  other arithmetic  57.7 us (13%)
  local copies, waits for them, and re-layouts  38.8 us (9%)
  between operations  23.3 us (5%)
    pallas_call x2, Pallas kernels, mlp_block(): call(mlp_kernel, (2 * per,), [whole((BL, half_width)), whole((BL, half_wi...  41 us
    pallas_call x2, Pallas kernels, attend_backward(): call(attend_back_kernel, (pairs + 2,), [whole((BL, D)), whole((BL, D)), p...  33.8 us
    ppermute x15, waiting for transfers between devices, swap_x(): return lax.ppermute(values, 'tensor', SWAP)  28.6 us
    ppermute x8, waiting for transfers between devices, gather_round(): other = lax.ppermute(held, 'dp', [(i, i ^ step) for i in range(count)])  23.1 us
    ppermute x8, starting transfers between devices, gather_round(): other = lax.ppermute(held, 'dp', [(i, i ^ step) for i in range(count)])  18.9 us
    pallas_call x2, Pallas kernels, attend_forward(): call(attend_kernel, (pairs,), [pl.BlockSpec((BL, D), lambda p, s: (block,...  18.8 us
    unnamed x168, local copies, waits for them, and re-layouts  18.4 us
    ppermute x15, starting transfers between devices, swap_x(): return lax.ppermute(values, 'tensor', SWAP)  16.5 us
  transfers between devices with their start and end apart: 50, of which 20 were waited for; matrix products, arithmetic and copies ran while one was open for 15% of the time, Pallas kernels for 32%

profile of v1, /device:TPU:0, one launch (start us, length us, event | category | flops | bytes accessed | tf_op | source)
XLA Modules:
  0.0 452.8 jit_solution(1884977660673298467)
XLA Ops:
  14.3 12.5 %conditional.5 = (bf16[256,512]{1,0:T(8,128)(2,1)}) conditional(s32[]{:T(128)} %bitcast.26, bf16[256,512]{1,0:T(8,128)(2,1)S(1)} %slice_bitcast_fusion.1, bf16[256,512]{1,0:T(8,128)(2,1)S(1)} %slice_bitcast_fusion.1, bf16[256,512]{1,0:T(8,128)(2,1)S(1)} %slice_bitcast_fusion.1, ...), branch_computations={%region_1.2_spmd, %region_2.3_spmd, %region_3.4_spmd, %region_4.5_... | conditional | bytes 1048624 | solution.py:221
  14.3 7.7 %collective-permute-start.2 = (bf16[256,512]{1,0:T(8,128)(2,1)S(1)}, bf16[256,512]{1,0:T(8,128)(2,1)}, u32[]{:S(2)}, u32[]{:S(2)}) collective-permute-start(bf16[256,512]{1,0:T(8,128)(2,1)S(1)} %param.2), channel_id=1, source_target_pairs={{0,24},{2,26},{4,28},{6,30},{1,25},{3,27},{5,29},{7,31}} | collective-permute-start | bytes 786440 | tf_op jit(solution)/shard_map/cond/branch_2_fun/ppermute | solution.py:219
  22.0 4.8 %collective-permute-done.2 = bf16[256,512]{1,0:T(8,128)(2,1)} collective-permute-done((bf16[256,512]{1,0:T(8,128)(2,1)S(1)}, bf16[256,512]{1,0:T(8,128)(2,1)}, u32[]{:S(2)}, u32[]{:S(2)}) %collective-permute-start.2) | collective-permute-done | bytes 262176 | tf_op jit(solution)/shard_map/cond/branch_2_fun/ppermute | solution.py:219
  26.8 1.7 fusion.33
  36.5 1.6 reshape.453
  40.3 5.6 %collective-permute-start.41 = (bf16[256,1024]{1,0:T(8,128)(2,1)}, bf16[256,1024]{1,0:T(8,128)(2,1)}, u32[]{:S(2)}, u32[]{:S(2)}) collective-permute-start(bf16[256,1024]{1,0:T(8,128)(2,1)} %slice.180), channel_id=1, source_target_pairs={{0,16},{2,18},{4,20},{6,22},{8,24},{10,26},{12,28},{14,30},{16,0},... | collective-permute-start | bytes 1572872 | tf_op jit(solution)/shard_map/ppermute | solution.py:228
  46.1 3.6 fusion.17
  49.7 4.6 %scan_kernel.1 = (f32[128,8,128]{2,1,0:T(8,128)S(1)}, f32[16,8,128]{2,1,0:T(8,128)S(1)}, f32[16,8,128]{2,1,0:T(8,128)S(1)}) custom-call(s32[1025]{0:T(1024)S(1)} %pad_add_fusion.seg_ref, f32[512,8,128]{2,1,0:T(8,128)S(1)} %bitcast.196, f32[16,8,128]{2,1,0:T(8,128)S(1)} %get-tuple-element.358.rate_ref, f32[16,8,128]{2,1,0:T(8,128)S(1)} %get-tuple-element.359.c_ref), custom_call_target="tpu_custom_call" | custom-call | flops 4000000 | bytes 1000 | tf_op jit(solution)/shard_map/scan_kernel/pallas_call | solution.py:1309
  59.4 2.2 collective-permute-done.43
  63.1 9.2 %collective-permute-done.40 = bf16[256,1024]{1,0:T(8,128)(2,1)} collective-permute-done((bf16[256,1024]{1,0:T(8,128)(2,1)}, bf16[256,1024]{1,0:T(8,128)(2,1)}, u32[]{:S(2)}, u32[]{:S(2)}) %collective-permute-start.40) | collective-permute-done | bytes 524320 | tf_op jit(solution)/shard_map/ppermute | solution.py:228
  73.4 9.3 %collective-permute-done.44 = bf16[4,144,128]{2,1,0:T(8,128)(2,1)S(1)} collective-permute-done((bf16[4,144,128]{2,1,0:T(8,128)(2,1)S(1)}, bf16[4,144,128]{2,1,0:T(8,128)(2,1)S(1)}, u32[]{:S(2)}, u32[]{:S(2)}) %collective-permute-start.44) | collective-permute-done | bytes 147488 | tf_op jit(solution)/shard_map/ppermute | solution.py:103
  85.9 2.9 collective-permute-start.45
  89.9 18.8 %collective-permute-done.38 = f32[2,512]{1,0:T(2,128)S(1)} collective-permute-done((f32[2,512]{1,0:T(2,128)S(1)}, f32[2,512]{1,0:T(2,128)S(1)}, u32[]{:S(2)}, u32[]{:S(2)}) %collective-permute-start.38) | collective-permute-done | bytes 4128 | tf_op jit(solution)/shard_map/ppermute | solution.py:83
  109.8 3.5 join_scaled_kernel.1.hid_ref.refs_0_.refs_1_
  118.9 1.8 tail_kernel.1
  121.5 1.6 slice.153
  128.0 4.2 collective-permute-start.47
  132.2 3.7 collective-permute-start.48
  135.9 2.0 dynamic-slice_bitcast_fusion.1
  142.9 9.6 %attend_kernel.3 = (bf16[512,512]{1,0:T(8,128)(2,1)}, bf16[512,512]{1,0:T(8,128)(2,1)}, bf16[512,512]{1,0:T(8,128)(2,1)}, bf16[128,512]{1,0:T(8,128)(2,1)}, bf16...) custom-call(s32[16]{0:T(128)S(1)} %copy-done.21, ...), custom_call_target="tpu_custom_call" | custom-call | flops 8000000 | bytes 12000 | tf_op jit(solution)/shard_map/attend_kernel/pallas_call | solution.py:696
  153.0 9.2 %attend_kernel.2 = (bf16[512,512]{1,0:T(8,128)(2,1)}, bf16[512,512]{1,0:T(8,128)(2,1)}, bf16[512,512]{1,0:T(8,128)(2,1)}, bf16[128,512]{1,0:T(8,128)(2,1)}, bf16...) custom-call(s32[16]{0:T(128)S(1)} %copy-done.21, ...), custom_call_target="tpu_custom_call" | custom-call | flops 8000000 | bytes 12000 | tf_op jit(solution)/shard_map/attend_kernel/pallas_call | solution.py:696
  163.8 3.2 join_kernel.2.tok_ref
  167.0 5.5 %sens_kernel.1 = (f32[16,8,128]{2,1,0:T(8,128)S(1)}, f32[16,8,128]{2,1,0:T(8,128)S(1)}) custom-call(s32[1025]{0:T(1024)S(1)} %pad_add_fusion.seg_ref, f32[512,8,128]{2,1,0:T(8,128)S(1)} %bitcast.197, f32[16,8,128]{2,1,0:T(8,128)S(1)} %get-tuple-element.216.start_ref, f32[16,8,128]{2,1,0:T(8,128)S(1)} %get-tuple-element.358.rate_ref), custom_call_target="tpu_custom_call" | custom-call | flops 6000000 | bytes 1000 | tf_op jit(solution)/shard_map/sens_kernel/pallas_call | solution.py:1344
  172.5 3.2 join_kernel.3.cot_ref.g0.g1
  175.7 2.7 collective-permute-done.50.other_ref
  178.4 2.9 maximum_select_fusion.woo_ref
  181.3 1.6 copy-done.1
  184.1 14.8 %mlp_kernel.2 = (f32[512,1024]{1,0:T(8,128)}, bf16[512,1024]{1,0:T(8,128)(2,1)S(1)}, bf16[512,2048]{1,0:T(8,128)(2,1)}, bf16[512,2048]{1,0:T(8,128)(2,1)S(1)}, bf16[512,1024]{1,0:T(8,128)(2,1)}) custom-call(s32[16]{0:T(128)S(1)} %copy-done.21, bf16[512,512]{1,0:T(8,128)(2,1)} %get-tuple-element.214.own_ref.refs_11_, ...), custom_call_target="tpu_custom_call" | custom-call | flops 8000000 | bytes 24000 | tf_op jit(solution)/shard_map/mlp_kernel/pallas_call | solution.py:1060
  199.2 26.3 %mlp_kernel.3 = (f32[512,1024]{1,0:T(8,128)}, bf16[512,1024]{1,0:T(8,128)(2,1)S(1)}, bf16[512,2048]{1,0:T(8,128)(2,1)}, bf16[512,2048]{1,0:T(8,128)(2,1)S(1)}, bf16[512,1024]{1,0:T(8,128)(2,1)}) custom-call(s32[16]{0:T(128)S(1)} %copy-done.21, bf16[512,512]{1,0:T(8,128)(2,1)} %get-tuple-element.215.own_ref.refs_17_, ...), custom_call_target="tpu_custom_call" | custom-call | flops 8000000 | bytes 24000 | tf_op jit(solution)/shard_map/mlp_kernel/pallas_call | solution.py:1060
  225.5 1.6 copy-done.12
  227.1 13.1 %mlp_grad_kernel.1 = bf16[4,1024,1024]{2,1,0:T(8,128)(2,1)} custom-call(s32[16]{0:T(128)S(1)} %copy-done.21, bf16[512,1024]{1,0:T(8,128)(2,1)S(1)} %get-tuple-element.227.h0, bf16[512,1024]{1,0:T(8,128)(2,1)S(1)} %get-tuple-element.229.h1, bf16[1024,1024]{1,0:T(8,128)(2,1)S(1)} %copy-done, bf16[1024,1024]{1,0:T(8,128)(2,1)S(1)} %copy-done, ...), custom_call_target="tpu_custom_call" | custom-call | flops 8600000 | bytes 20000 | tf_op jit(solution)/shard_map/mlp_grad_kernel/pallas_call | solution.py:1124
  240.2 1.8 collective-permute-start.56
  242.0 17.0 %attend_back_kernel.2 = (bf16[512,1024]{1,0:T(8,128)(2,1)}, f32[512,1024]{1,0:T(8,128)}, f32[1,1024]{1,0:T(1,128)S(1)}, bf16[512,512]{1,0:T(8,128)(2,1)}, bf16[5...) custom-call(s32[16]{0:T(128)S(1)} %copy-done.21, ...), custom_call_target="tpu_custom_call" | custom-call | flops 12000000 | bytes 20000 | tf_op jit(solution)/shard_map/attend_back_kernel/pallas_call | solution.py:871
  259.1 10.9 %mlp_out_kernel.1 = (bf16[1024,512]{1,0:T(8,128)(2,1)S(1)}, f32[1024,512]{1,0:T(8,128)}) custom-call(s32[16]{0:T(128)S(1)} %copy-done.21, bf16[512,2048]{1,0:T(8,128)(2,1)} %get-tuple-element.243.a0, bf16[512,2048]{1,0:T(8,128)(2,1)} %get-tuple-element.232.a1, bf16[4,1024,1024]{2,1,0:T(8,128)(2,1)} %bitcast.233, bf16[4,1024,1024]{2,1,0:T(8,128)(2,1)} %bitcast.234, ...), custom_call_target="tpu_custom_call" | custom-call | flops 4400000 | bytes 12000 | tf_op jit(solution)/shard_map/mlp_out_kernel/pallas_call | solution.py:1185
  271.3 16.8 %attend_back_kernel.3 = (bf16[512,1024]{1,0:T(8,128)(2,1)}, f32[512,1024]{1,0:T(8,128)}, f32[1,1024]{1,0:T(1,128)S(1)}, bf16[512,512]{1,0:T(8,128)(2,1)}, bf16[5...) custom-call(s32[16]{0:T(128)S(1)} %copy-done.21, ...), custom_call_target="tpu_custom_call" | custom-call | flops 12000000 | bytes 20000 | tf_op jit(solution)/shard_map/attend_back_kernel/pallas_call | solution.py:871
  288.1 1.8 collective-permute-start.57
  292.5 5.6 %collective-permute-done.57 = bf16[128,512]{1,0:T(8,128)(2,1)S(1)} collective-permute-done((bf16[128,512]{1,0:T(8,128)(2,1)S(1)}, bf16[128,512]{1,0:T(8,128)(2,1)S(1)}, u32[]{:S(2)}, u32[]{:S(2)}) %collective-permute-start.57) | collective-permute-done | bytes 131104 | tf_op jit(solution)/shard_map/ppermute | solution.py:83
  299.8 1.9 back_total_kernel.1
  305.3 10.6 %collective-permute-start.61 = (bf16[2,128,128]{2,1,0:T(8,128)(2,1)S(1)}, bf16[2,128,128]{2,1,0:T(8,128)(2,1)S(1)}, u32[]{:S(2)}, u32[]{:S(2)}) collective-permute-start(bf16[2,128,128]{2,1,0:T(8,128)(2,1)S(1)} %maximum_select_fusion.10), channel_id=1, source_target_pairs={{0,4},{2,6},{4,0},{6,2},{8,12},{10,14},{12,8},{14,10},{16,20},{18,... | collective-permute-start | bytes 196616 | tf_op jit(solution)/shard_map/ppermute | solution.py:103
  315.9 11.8 %attn_grad_kernel.1 = bf16[4,1024,512]{2,1,0:T(8,128)(2,1)} custom-call(s32[16]{0:T(128)S(1)} %copy-done.21, bf16[1024,1024]{1,0:T(8,128)(2,1)} %join_scaled_kernel.1.hid_ref.refs_0_.refs_1_, bf16[1024,1024]{1,0:T(8,128)(2,1)} %join_scaled_kernel.1.hid_ref.refs_0_.refs_1_, bf16[256,1024]{1,0:T(8,128)(2,1)} %bitcast.201, bf16[256,1024]{1,0:T(8,128)(2,1)} %bitcast.202, ...), custom_call_target="tpu_custom_call" | custom-call | flops 4600000 | bytes 14000 | tf_op jit(solution)/shard_map/attn_grad_kernel/pallas_call | solution.py:986
  328.4 3.2 dynamic-slice_bitcast_fusion
  338.1 1.7 collective-permute-start.63
  339.9 2.4 constant_dynamic-slice_fusion.3
  342.3 8.4 %collective-permute-done.63 = bf16[4,128,128]{2,1,0:T(8,128)(2,1)S(1)} collective-permute-done((bf16[4,128,128]{2,1,0:T(8,128)(2,1)S(1)}, bf16[4,128,128]{2,1,0:T(8,128)(2,1)S(1)}, u32[]{:S(2)}, u32[]{:S(2)}) %collective-permute-start.63) | collective-permute-done | bytes 131104 | tf_op jit(solution)/shard_map/ppermute | solution.py:103
  351.4 2.1 fusion.31
  354.1 1.7 reduce.1
  359.3 3.4 sens_tail_kernel.1
  362.7 1.6 collective-permute-start.64
  367.7 2.7 collective-permute-done.64
  371.8 2.2 fusion.28
  375.5 1.6 collective-permute-start.77
  377.2 5.2 %back_scan_kernel.1 = (f32[512,8,128]{2,1,0:T(8,128)S(1)}, f32[16,8,128]{2,1,0:T(8,128)S(1)}) custom-call(s32[1025]{0:T(1024)S(1)} %pad_add_fusion.seg_ref, s32[16]{0:T(128)S(1)} %get-tuple-element.351.use_ref, bf16[16,128,128]{2,1,0:T(8,128)(2,1)S(1)} %maximum_select_fusion.2.all_ref, f32[128,8,128]{2,1,0:T(8,128)S(1)} %bitcast.205, ...), custom_call_target="tpu_custom_call" | custom-call | flops 4000000 | bytes 1000 | tf_op jit(solution)/shard_map/back_scan_kernel/pallas_call | solution.py:1477
  384.4 2.3 fusion.9
  390.7 3.8 fusion.8
  394.5 7.4 %collective-permute-done.70 = bf16[256,512]{1,0:T(8,128)(2,1)S(1)} collective-permute-done((bf16[256,512]{1,0:T(8,128)(2,1)S(1)}, bf16[256,512]{1,0:T(8,128)(2,1)S(1)}, u32[]{:S(2)}, u32[]{:S(2)}) %collective-permute-start.70) | collective-permute-done | bytes 262176 | tf_op jit(solution)/shard_map/ppermute | solution.py:327
  403.1 3.7 collective-permute-start.71
  407.5 2.7 fusion.16
  410.2 4.5 collective-permute-done.78
  416.2 2.0 collective-permute-start.72
  420.2 5.4 %fusion.51 = (bf16[1,256,2048]{2,1,0:T(8,128)(2,1)}, f32[1,256,2048]{2,1,0:T(8,128)}, f32[1,256,2048]{2,1,0:T(8,128)}, f32[1,256,2048]{2,1,0:T(8,128)}, f32[1,256,2048]{2,1,0:T(8,128)}) fusion(f32[1,256,2048]{2,1,0:T(8,128)S(1)} %copy-done.37, f32[]{:T(128)} %bitcast.77, f32[1,256,2048]{2,1,0:T(8,128)S(1)} %copy-done.45, f32[1,256,2048]{2,1,0:T(8,128)S(1)} %copy-done.46, ...), kind=kLoop, calls=%fused_computation.143 | loop fusion | flops 11010048 | bytes 16777220 | tf_op jit(solution)/shard_map/convert_element_type | solution.py:1572
  425.6 2.3 collective-permute-done.80
  430.7 10.2 %conditional.6 = (bf16[256,512]{1,0:T(8,128)(2,1)}) conditional(s32[]{:T(128)} %bitcast.26, bf16[256,512]{1,0:T(8,128)(2,1)S(1)} %get-tuple-element.305, bf16[256,512]{1,0:T(8,128)(2,1)S(1)} %get-tuple-element.305, bf16[256,512]{1,0:T(8,128)(2,1)S(1)} %get-tuple-element.305, ...), branch_computations={%region_22.23_spmd, %region_23.24_spmd, %region_24.25_spmd, %regio... | conditional | bytes 1048624
  432.0 8.9 %collective-permute-done.20 = bf16[256,512]{1,0:T(8,128)(2,1)} collective-permute-done((bf16[256,512]{1,0:T(8,128)(2,1)S(1)}, bf16[256,512]{1,0:T(8,128)(2,1)}, u32[]{:S(2)}, u32[]{:S(2)}) %collective-permute-start.20) | collective-permute-done | bytes 262176 | tf_op jit(solution)/shard_map/cond/branch_2_fun/ppermute | solution.py:219
  441.9 3.9 fusion.53
  (325 shorter events, 85.7 us)
Async XLA Ops:
  7.2 21.4 %copy-start.2 = (bf16[1,1024,512]{2,1,0:T(8,128)(2,1)S(1)}, bf16[1,1024,512]{2,1,0:T(8,128)(2,1)}, u32[]{:S(2)}) copy-start(bf16[1,1024,512]{2,1,0:T(8,128)(2,1)} %param.54) | copy-start | bytes 3145732
  7.2 128.7 %all-gather.3.cloned.1.call-start = ((), (), s32[]{:S(2)}) async-start(), calls=%async_computation.1 | async-start | bytes 4456448 | tf_op jit(solution)/shard_map/all_gather | solution.py:1273
  10.7 19.7 %copy-start.66 = (s32[1,1024]{1,0:T(1,128)S(1)}, s32[1,1024]{1,0:T(1,128)}, u32[]{:S(2)}) copy-start(s32[1,1024]{1,0:T(1,128)} %param.56) | copy-start | bytes 12292
  10.7 22.1 %copy-start.52 = (f32[3,512,16]{1,2,0:T(8,128)S(1)}, f32[3,512,16]{1,2,0:T(8,128)}, u32[]{:S(2)}) copy-start(f32[3,512,16]{1,2,0:T(8,128)} %param.64) | copy-start | bytes 294916
  10.7 24.2 %copy-start.36 = (f32[1,256,2048]{2,1,0:T(8,128)S(1)}, f32[1,256,2048]{2,1,0:T(8,128)}, u32[]{:S(2)}) copy-start(f32[1,256,2048]{2,1,0:T(8,128)} %param.61) | copy-start | bytes 6291460
  14.3 12.5 %collective-permute-start.2 = (bf16[256,512]{1,0:T(8,128)(2,1)S(1)}, bf16[256,512]{1,0:T(8,128)(2,1)}, u32[]{:S(2)}, u32[]{:S(2)}) collective-permute-start(bf16[256,512]{1,0:T(8,128)(2,1)S(1)} %param.2), channel_id=1, source_target_pairs={{0,24},{2,26},{4,28},{6,30},{1,25},{3,27},{5,29},{7,31}} | collective-permute-start | bytes 786440 | tf_op jit(solution)/shard_map/cond/branch_2_fun/ppermute | solution.py:219
  28.5 152.8 %all-gather.5.cloned.1.call-start = ((), (), s32[]{:S(2)}) async-start(), calls=%async_computation.2 | async-start | bytes 8912896 | tf_op jit(solution)/shard_map/all_gather | solution.py:1334
  28.8 11.4 %collective-permute-start.37 = (f32[1024]{0:T(1024)S(1)}, f32[1024]{0:T(1024)S(1)}, u32[]{:S(2)}, u32[]{:S(2)}) collective-permute-start(f32[1024]{0:T(1024)S(1)} %fusion.10), channel_id=1, source_target_pairs={{0,1},{1,0},{2,3},{3,2},{4,5},{5,4},{6,7},{7,6},{8,9},{9,8},{10,11... | collective-permute-start | bytes 12296 | tf_op jit(solution)/shard_map/ppermute | solution.py:83
  30.9 8.0 %collective-permute-start.39 = (s32[128]{0:T(128)S(1)}, s32[128]{0:T(128)S(1)}, u32[]{:S(2)}, u32[]{:S(2)}) collective-permute-start(s32[128]{0:T(128)S(1)} %get-tuple-element.346), channel_id=1, source_target_pairs={{0,2},{2,4},{4,6},{6,8},{8,10},{10,12},{12,14},{14,16},{16,18},{18... | collective-permute-start | bytes 1544 | tf_op jit(solution)/shard_map/ppermute | solution.py:1278
  32.2 30.4 %collective-permute-start.36 = (bf16[1024,512]{1,0:T(8,128)(2,1)S(1)}, bf16[1024,512]{1,0:T(8,128)(2,1)}, u32[]{:S(2)}, u32[]{:S(2)}) collective-permute-start(bf16[1024,512]{1,0:T(8,128)(2,1)S(1)} %bitcast.193), channel_id=1, source_target_pairs={{0,1},{1,0},{2,3},{3,2},{4,5},{5,4},{6,7},{7,6},{8,9},{9,8},{10,11... | collective-permute-start | bytes 3145736 | tf_op jit(solution)/shard_map/ppermute | solution.py:83
  40.3 32.0 %collective-permute-start.40 = (bf16[256,1024]{1,0:T(8,128)(2,1)}, bf16[256,1024]{1,0:T(8,128)(2,1)}, u32[]{:S(2)}, u32[]{:S(2)}) collective-permute-start(bf16[256,1024]{1,0:T(8,128)(2,1)} %slice.180), channel_id=1, source_target_pairs={{0,8},{2,10},{4,12},{6,14},{8,0},{10,2},{12,4},{14,6},{16,24},{18,... | collective-permute-start | bytes 1572872 | tf_op jit(solution)/shard_map/ppermute | solution.py:228
  40.3 31.9 %collective-permute-start.41 = (bf16[256,1024]{1,0:T(8,128)(2,1)}, bf16[256,1024]{1,0:T(8,128)(2,1)}, u32[]{:S(2)}, u32[]{:S(2)}) collective-permute-start(bf16[256,1024]{1,0:T(8,128)(2,1)} %slice.180), channel_id=1, source_target_pairs={{0,16},{2,18},{4,20},{6,22},{8,24},{10,26},{12,28},{14,30},{16,0},... | collective-permute-start | bytes 1572872 | tf_op jit(solution)/shard_map/ppermute | solution.py:228
  46.0 42.9 %copy-start.62 = (f32[1024]{0:T(1024)}, f32[1024]{0:T(1024)S(1)}, u32[]{:S(2)}) copy-start(f32[1024]{0:T(1024)S(1)} %add_rsqrt_fusion) | copy-start | bytes 12292
  49.7 117.3 %copy-start.3 = (f32[2,512,4,128]{3,2,0,1:T(4,128)}, f32[2,512,4,128]{3,2,0,1:T(4,128)S(1)}, u32[]{:S(2)}) copy-start(f32[2,512,4,128]{3,2,0,1:T(4,128)S(1)} %fusion.17) | copy-start | bytes 6291460
  55.2 1.6 collective-permute-start.42
  56.9 4.7 %collective-permute-start.43 = (bf16[2,144,128]{2,1,0:T(8,128)(2,1)S(1)}, bf16[2,144,128]{2,1,0:T(8,128)(2,1)}, u32[]{:S(2)}, u32[]{:S(2)}) collective-permute-start(bf16[2,144,128]{2,1,0:T(8,128)(2,1)S(1)} %maximum_select_fusion.9), channel_id=1, source_target_pairs={{0,4},{2,6},{4,0},{6,2},{8,12},{10,14},{12,8},{14,10},{16,20},{18,... | collective-permute-start | bytes 221192 | tf_op jit(solution)/shard_map/ppermute | solution.py:103
  58.1 25.3 %copy-start.42 = (bf16[256,2048]{1,0:T(8,128)(2,1)S(1)}, bf16[256,2048]{1,0:T(8,128)(2,1)}, u32[]{:S(2)}) copy-start(bf16[256,2048]{1,0:T(8,128)(2,1)} %convert_bitcast_fusion) | copy-start | bytes 3145732
  62.6 20.0 %collective-permute-start.44 = (bf16[4,144,128]{2,1,0:T(8,128)(2,1)S(1)}, bf16[4,144,128]{2,1,0:T(8,128)(2,1)S(1)}, u32[]{:S(2)}, u32[]{:S(2)}) collective-permute-start(bf16[4,144,128]{2,1,0:T(8,128)(2,1)S(1)} %maximum_select_fusion.7), channel_id=1, source_target_pairs={{0,8},{2,10},{4,12},{6,14},{8,0},{10,2},{12,4},{14,6},{16,24},{18,... | collective-permute-start | bytes 442376 | tf_op jit(solution)/shard_map/ppermute | solution.py:103
  72.2 16.6 %copy-start.69 = (f32[2,512]{1,0:T(2,128)S(1)}, f32[2,512]{1,0:T(2,128)}, u32[]{:S(2)}) copy-start(f32[2,512]{1,0:T(2,128)} %param.67) | copy-start | bytes 12292
  72.2 36.5 %copy-start.21 = (s32[16]{0:T(128)S(1)}, s32[16]{0:T(128)}, u32[]{:S(2)}) copy-start(s32[16]{0:T(128)} %get-tuple-element.204.host_ref) | copy-start | bytes 196
  84.3 289.7 %reduce-scatter.2.cloned.1.call-start = ((), (), s32[]{:S(2)}) async-start(), calls=%async_computation.3 | async-start | bytes 8912896 | tf_op jit(solution)/shard_map/reduce_scatter | solution.py:1412
  84.3 30.2 %collective-permute-start.46 = (bf16[1024,512]{1,0:T(8,128)(2,1)}, bf16[1024,512]{1,0:T(8,128)(2,1)}, u32[]{:S(2)}, u32[]{:S(2)}) collective-permute-start(bf16[1024,512]{1,0:T(8,128)(2,1)} %bitcast.207), channel_id=1, source_target_pairs={{0,1},{1,0},{2,3},{3,2},{4,5},{5,4},{6,7},{7,6},{8,9},{9,8},{10,11... | collective-permute-start | bytes 3145736 | tf_op jit(solution)/shard_map/ppermute | solution.py:83
  85.9 27.4 %collective-permute-start.45 = (bf16[8,144,128]{2,1,0:T(8,128)(2,1)}, bf16[8,144,128]{2,1,0:T(8,128)(2,1)}, u32[]{:S(2)}, u32[]{:S(2)}) collective-permute-start(bf16[8,144,128]{2,1,0:T(8,128)(2,1)} %maximum_select_fusion.3), channel_id=1, source_target_pairs={{0,16},{2,18},{4,20},{6,22},{8,24},{10,26},{12,28},{14,30},{16,0},... | collective-permute-start | bytes 884744 | tf_op jit(solution)/shard_map/ppermute | solution.py:103
  88.8 20.0 %collective-permute-start.38 = (f32[2,512]{1,0:T(2,128)S(1)}, f32[2,512]{1,0:T(2,128)S(1)}, u32[]{:S(2)}, u32[]{:S(2)}) collective-permute-start(f32[2,512]{1,0:T(2,128)S(1)} %copy-done.69), channel_id=1, source_target_pairs={{0,1},{1,0},{2,3},{3,2},{4,5},{5,4},{6,7},{7,6},{8,9},{9,8},{10,11... | collective-permute-start | bytes 12296 | tf_op jit(solution)/shard_map/ppermute | solution.py:83
  118.8 20.5 %copy-start.76 = (s32[128]{0:T(128)S(1)}, s32[128]{0:T(128)}, u32[]{:S(2)}) copy-start(s32[128]{0:T(128)} %get-tuple-element.345) | copy-start | bytes 1540
  118.9 21.5 %copy-start.80 = (s32[128]{0:T(128)S(1)}, s32[128]{0:T(128)}, u32[]{:S(2)}) copy-start(s32[128]{0:T(128)} %copy-done.79) | copy-start | bytes 1540
  123.1 14.8 %collective-permute-start.49 = (bf16[1,128,512]{2,1,0:T(8,128)(2,1)}, bf16[1,128,512]{2,1,0:T(8,128)(2,1)}, u32[]{:S(2)}, u32[]{:S(2)}) collective-permute-start(bf16[1,128,512]{2,1,0:T(8,128)(2,1)} %slice.153), channel_id=1, source_target_pairs={{0,1},{1,0},{2,3},{3,2},{4,5},{5,4},{6,7},{7,6},{8,9},{9,8},{10,11... | collective-permute-start | bytes 393224 | tf_op jit(solution)/shard_map/ppermute | solution.py:83
  128.0 12.3 %collective-permute-start.47 = (bf16[128,512]{1,0:T(8,128)(2,1)}, bf16[128,512]{1,0:T(8,128)(2,1)}, u32[]{:S(2)}, u32[]{:S(2)}) collective-permute-start(bf16[128,512]{1,0:T(8,128)(2,1)} %bitcast.189), channel_id=1, source_target_pairs={{0,2},{1,3},{2,4},{3,5},{4,6},{5,7},{6,8},{7,9},{8,10},{9,11},{10,... | collective-permute-start | bytes 393224 | tf_op jit(solution)/shard_map/ppermute | solution.py:345
  132.2 8.2 %collective-permute-start.48 = (bf16[128,512]{1,0:T(8,128)(2,1)}, bf16[128,512]{1,0:T(8,128)(2,1)}, u32[]{:S(2)}, u32[]{:S(2)}) collective-permute-start(bf16[128,512]{1,0:T(8,128)(2,1)} %bitcast.189), channel_id=1, source_target_pairs={{0,3},{1,2},{2,5},{3,4},{4,7},{5,6},{6,9},{7,8},{8,11},{9,10},{10,... | collective-permute-start | bytes 393224 | tf_op jit(solution)/shard_map/ppermute | solution.py:345
  137.9 25.9 %collective-permute-start.52 = (bf16[512,512]{1,0:T(8,128)(2,1)}, bf16[512,512]{1,0:T(8,128)(2,1)}, u32[]{:S(2)}, u32[]{:S(2)}) collective-permute-start(bf16[512,512]{1,0:T(8,128)(2,1)} %dynamic-slice_bitcast_fusion.1), channel_id=1, source_target_pairs={{0,1},{1,0},{2,3},{3,2},{4,5},{5,4},{6,7},{7,6},{8,9},{9,8},{10,11... | collective-permute-start | bytes 1572872 | tf_op jit(solution)/shard_map/ppermute | solution.py:83
  152.4 23.3 %collective-permute-start.51 = (bf16[512,512]{1,0:T(8,128)(2,1)}, bf16[512,512]{1,0:T(8,128)(2,1)}, u32[]{:S(2)}, u32[]{:S(2)}) collective-permute-start(bf16[512,512]{1,0:T(8,128)(2,1)} %get-tuple-element.215.own_ref.refs_17_), channel_id=1, source_target_pairs={{0,1},{1,0},{2,3},{3,2},{4,5},{5,4},{6,7},{7,6},{8,9},{9,8},{10,11... | collective-permute-start | bytes 1572872 | tf_op jit(solution)/shard_map/ppermute | solution.py:83
  162.3 16.1 %collective-permute-start.50 = (bf16[512,512]{1,0:T(8,128)(2,1)}, bf16[512,512]{1,0:T(8,128)(2,1)}, u32[]{:S(2)}, u32[]{:S(2)}) collective-permute-start(bf16[512,512]{1,0:T(8,128)(2,1)} %get-tuple-element.214.own_ref.refs_11_), channel_id=1, source_target_pairs={{0,1},{1,0},{2,3},{3,2},{4,5},{5,4},{6,7},{7,6},{8,9},{9,8},{10,11... | collective-permute-start | bytes 1572872 | tf_op jit(solution)/shard_map/ppermute | solution.py:83
  163.8 14.6 %collective-permute-start.53 = (bf16[512,512]{1,0:T(8,128)(2,1)}, bf16[512,512]{1,0:T(8,128)(2,1)}, u32[]{:S(2)}, u32[]{:S(2)}) collective-permute-start(bf16[512,512]{1,0:T(8,128)(2,1)} %collective-permute-done.52), channel_id=1, source_target_pairs={{0,2},{2,0},{4,6},{6,4},{8,10},{10,8},{12,14},{14,12},{16,18},{18,... | collective-permute-start | bytes 1572872 | tf_op jit(solution)/shard_map/ppermute | solution.py:1378
  198.9 26.6 %copy-start.11 = (bf16[512,2048]{1,0:T(8,128)(2,1)S(1)}, bf16[512,2048]{1,0:T(8,128)(2,1)}, u32[]{:S(2)}) copy-start(bf16[512,2048]{1,0:T(8,128)(2,1)} %get-tuple-element.243.a0) | copy-start | bytes 6291460
  198.9 41.3 %collective-permute-start.54 = (bf16[512,1024]{1,0:T(8,128)(2,1)}, bf16[512,1024]{1,0:T(8,128)(2,1)}, u32[]{:S(2)}, u32[]{:S(2)}) collective-permute-start(bf16[512,1024]{1,0:T(8,128)(2,1)} %get-tuple-element.226.own_ref), channel_id=1, source_target_pairs={{0,1},{1,0},{2,3},{3,2},{4,5},{5,4},{6,7},{7,6},{8,9},{9,8},{10,11... | collective-permute-start | bytes 3145736 | tf_op jit(solution)/shard_map/ppermute | solution.py:83
  240.2 30.1 %collective-permute-start.56 = (bf16[512,1024]{1,0:T(8,128)(2,1)}, bf16[512,1024]{1,0:T(8,128)(2,1)S(1)}, u32[]{:S(2)}, u32[]{:S(2)}) collective-permute-start(bf16[512,1024]{1,0:T(8,128)(2,1)} %get-tuple-element.250.own_ref), channel_id=1, source_target_pairs={{0,1},{1,0},{2,3},{3,2},{4,5},{5,4},{6,7},{7,6},{8,9},{9,8},{10,11... | collective-permute-start | bytes 3145736 | tf_op jit(solution)/shard_map/ppermute | solution.py:83
  270.0 29.8 %collective-permute-start.55 = (bf16[1024,512]{1,0:T(8,128)(2,1)S(1)}, bf16[1024,512]{1,0:T(8,128)(2,1)}, u32[]{:S(2)}, u32[]{:S(2)}) collective-permute-start(bf16[1024,512]{1,0:T(8,128)(2,1)S(1)} %get-tuple-element.246), channel_id=1, source_target_pairs={{0,1},{1,0},{2,3},{3,2},{4,5},{5,4},{6,7},{7,6},{8,9},{9,8},{10,11... | collective-permute-start | bytes 3145736 | tf_op jit(solution)/shard_map/ppermute | solution.py:83
  288.1 10.0 %collective-permute-start.57 = (bf16[128,512]{1,0:T(8,128)(2,1)S(1)}, bf16[128,512]{1,0:T(8,128)(2,1)S(1)}, u32[]{:S(2)}, u32[]{:S(2)}) collective-permute-start(bf16[128,512]{1,0:T(8,128)(2,1)S(1)} %get-tuple-element.260), channel_id=1, source_target_pairs={{0,1},{1,0},{2,3},{3,2},{4,5},{5,4},{6,7},{7,6},{8,9},{9,8},{10,11... | collective-permute-start | bytes 393224 | tf_op jit(solution)/shard_map/ppermute | solution.py:83
  289.9 8.3 %collective-permute-start.58 = (bf16[128,512]{1,0:T(8,128)(2,1)S(1)}, bf16[128,512]{1,0:T(8,128)(2,1)}, u32[]{:S(2)}, u32[]{:S(2)}) collective-permute-start(bf16[128,512]{1,0:T(8,128)(2,1)S(1)} %convert_element_type.324), channel_id=1, source_target_pairs={{2,0},{3,1},{4,2},{5,3},{6,4},{7,5},{8,6},{9,7},{10,8},{11,9},{12,... | collective-permute-start | bytes 393224 | tf_op jit(solution)/shard_map/ppermute | solution.py:345
  291.2 7.4 %collective-permute-start.59 = (bf16[128,512]{1,0:T(8,128)(2,1)S(1)}, bf16[128,512]{1,0:T(8,128)(2,1)}, u32[]{:S(2)}, u32[]{:S(2)}) collective-permute-start(bf16[128,512]{1,0:T(8,128)(2,1)S(1)} %get-tuple-element.262), channel_id=1, source_target_pairs={{2,1},{3,0},{4,3},{5,2},{6,5},{7,4},{8,7},{9,6},{10,9},{11,8},{12,... | collective-permute-start | bytes 393224 | tf_op jit(solution)/shard_map/ppermute | solution.py:345
  303.2 2.2 collective-permute-start.60
  305.3 22.4 %collective-permute-start.61 = (bf16[2,128,128]{2,1,0:T(8,128)(2,1)S(1)}, bf16[2,128,128]{2,1,0:T(8,128)(2,1)S(1)}, u32[]{:S(2)}, u32[]{:S(2)}) collective-permute-start(bf16[2,128,128]{2,1,0:T(8,128)(2,1)S(1)} %maximum_select_fusion.10), channel_id=1, source_target_pairs={{0,4},{2,6},{4,0},{6,2},{8,12},{10,14},{12,8},{14,10},{16,20},{18,... | collective-permute-start | bytes 196616 | tf_op jit(solution)/shard_map/ppermute | solution.py:103
  331.6 19.8 %collective-permute-start.62 = (bf16[8,256,512]{2,1,0:T(8,128)(2,1)}, bf16[8,256,512]{2,1,0:T(8,128)(2,1)}, u32[]{:S(2)}, u32[]{:S(2)}) collective-permute-start(bf16[8,256,512]{2,1,0:T(8,128)(2,1)} %dynamic-slice_bitcast_fusion), channel_id=1, source_target_pairs={{0,2},{2,0},{4,6},{6,4},{8,10},{10,8},{12,14},{14,12},{16,18},{18,... | collective-permute-start | bytes 6291464 | tf_op jit(solution)/shard_map/ppermute | solution.py:315
  335.0 48.1 %collective-permute-start.69 = (bf16[512,512]{1,0:T(8,128)(2,1)}, bf16[512,512]{1,0:T(8,128)(2,1)}, u32[]{:S(2)}, u32[]{:S(2)}) collective-permute-start(bf16[512,512]{1,0:T(8,128)(2,1)} %get-tuple-element.296), channel_id=1, source_target_pairs={{0,1},{1,0},{2,3},{3,2},{4,5},{5,4},{6,7},{7,6},{8,9},{9,8},{10,11... | collective-permute-start | bytes 1572872 | tf_op jit(solution)/shard_map/ppermute | solution.py:83
  335.5 47.6 %collective-permute-start.68 = (bf16[512,512]{1,0:T(8,128)(2,1)}, bf16[512,512]{1,0:T(8,128)(2,1)}, u32[]{:S(2)}, u32[]{:S(2)}) collective-permute-start(bf16[512,512]{1,0:T(8,128)(2,1)} %get-tuple-element.295), channel_id=1, source_target_pairs={{0,1},{1,0},{2,3},{3,2},{4,5},{5,4},{6,7},{7,6},{8,9},{9,8},{10,11... | collective-permute-start | bytes 1572872 | tf_op jit(solution)/shard_map/ppermute | solution.py:83
  338.1 12.5 %collective-permute-start.63 = (bf16[4,128,128]{2,1,0:T(8,128)(2,1)S(1)}, bf16[4,128,128]{2,1,0:T(8,128)(2,1)S(1)}, u32[]{:S(2)}, u32[]{:S(2)}) collective-permute-start(bf16[4,128,128]{2,1,0:T(8,128)(2,1)S(1)} %copy-done.56), channel_id=1, source_target_pairs={{0,8},{2,10},{4,12},{6,14},{8,0},{10,2},{12,4},{14,6},{16,24},{18,... | collective-permute-start | bytes 393224 | tf_op jit(solution)/shard_map/ppermute | solution.py:103
  339.9 16.7 %copy-start.4 = (f32[2,512,4,128]{3,2,0,1:T(4,128)S(1)}, f32[2,512,4,128]{3,2,0,1:T(4,128)}, u32[]{:S(2)}) copy-start(f32[2,512,4,128]{3,2,0,1:T(4,128)} %copy-done.3) | copy-start | bytes 6291460
  353.5 12.8 %collective-permute-start.66 = (bf16[8,128,128]{2,1,0:T(8,128)(2,1)}, bf16[8,128,128]{2,1,0:T(8,128)(2,1)}, u32[]{:S(2)}, u32[]{:S(2)}) collective-permute-start(bf16[8,128,128]{2,1,0:T(8,128)(2,1)} %maximum_select_fusion.6), channel_id=1, source_target_pairs={{0,16},{2,18},{4,20},{6,22},{8,24},{10,26},{12,28},{14,30},{16,0},... | collective-permute-start | bytes 786440 | tf_op jit(solution)/shard_map/ppermute | solution.py:103
  362.7 7.7 %collective-permute-start.64 = (bf16[256,512]{1,0:T(8,128)(2,1)S(1)}, bf16[256,512]{1,0:T(8,128)(2,1)S(1)}, u32[]{:S(2)}, u32[]{:S(2)}) collective-permute-start(bf16[256,512]{1,0:T(8,128)(2,1)S(1)} %copy-done.59), channel_id=1, source_target_pairs={{0,8},{2,10},{8,16},{10,18},{16,24},{18,26},{24,28},{26,30},{28,20... | collective-permute-start | bytes 786440 | tf_op jit(solution)/shard_map/ppermute | solution.py:327
  364.4 7.4 %collective-permute-start.65 = (bf16[256,512]{1,0:T(8,128)(2,1)S(1)}, bf16[256,512]{1,0:T(8,128)(2,1)S(1)}, u32[]{:S(2)}, u32[]{:S(2)}) collective-permute-start(bf16[256,512]{1,0:T(8,128)(2,1)S(1)} %copy-done.58), channel_id=1, source_target_pairs={{8,0},{10,2},{16,8},{18,10},{24,16},{26,18},{28,24},{30,26},{20,28... | collective-permute-start | bytes 786440 | tf_op jit(solution)/shard_map/ppermute | solution.py:331
  374.0 32.8 %collective-permute-start.76 = (bf16[256,1024]{1,0:T(8,128)(2,1)}, bf16[256,1024]{1,0:T(8,128)(2,1)S(1)}, u32[]{:S(2)}, u32[]{:S(2)}) collective-permute-start(bf16[256,1024]{1,0:T(8,128)(2,1)} %reduce-scatter.2.cloned.1.call-done), channel_id=1, source_target_pairs={{0,8},{2,10},{4,12},{6,14},{8,0},{10,2},{12,4},{14,6},{16,24},{18,... | collective-permute-start | bytes 1572872 | tf_op jit(solution)/shard_map/ppermute | solution.py:228
  375.5 31.3 %collective-permute-start.77 = (bf16[256,1024]{1,0:T(8,128)(2,1)}, bf16[256,1024]{1,0:T(8,128)(2,1)S(1)}, u32[]{:S(2)}, u32[]{:S(2)}) collective-permute-start(bf16[256,1024]{1,0:T(8,128)(2,1)} %reduce-scatter.2.cloned.1.call-done), channel_id=1, source_target_pairs={{0,16},{2,18},{4,20},{6,22},{8,24},{10,26},{12,28},{14,30},{16,0},... | collective-permute-start | bytes 1572872 | tf_op jit(solution)/shard_map/ppermute | solution.py:228
  386.7 3.7 collective-permute-start.67
  388.2 6.3 %collective-permute-start.75 = (f32[34,512]{1,0:T(8,128)S(1)}, f32[34,512]{1,0:T(8,128)S(1)}, u32[]{:S(2)}, u32[]{:S(2)}) collective-permute-start(f32[34,512]{1,0:T(8,128)S(1)} %pad_maximum_fusion.3), channel_id=1, source_target_pairs={{0,2},{2,0},{4,6},{6,4},{8,10},{10,8},{12,14},{14,12},{16,18},{18,... | collective-permute-start | bytes 208904 | tf_op jit(solution)/shard_map/ppermute | solution.py:117
  388.3 13.7 %collective-permute-start.70 = (bf16[256,512]{1,0:T(8,128)(2,1)S(1)}, bf16[256,512]{1,0:T(8,128)(2,1)S(1)}, u32[]{:S(2)}, u32[]{:S(2)}) collective-permute-start(bf16[256,512]{1,0:T(8,128)(2,1)S(1)} %copy-done.61), channel_id=1, source_target_pairs={{0,8},{2,10},{8,16},{10,18},{16,24},{18,26},{24,28},{26,30},{28,20... | collective-permute-start | bytes 786440 | tf_op jit(solution)/shard_map/ppermute | solution.py:327
  390.4 24.4 %collective-permute-start.73 = (bf16[256,512]{1,0:T(8,128)(2,1)S(1)}, bf16[256,512]{1,0:T(8,128)(2,1)S(1)}, u32[]{:S(2)}, u32[]{:S(2)}) collective-permute-start(bf16[256,512]{1,0:T(8,128)(2,1)S(1)} %copy-done.60), channel_id=1, source_target_pairs={{8,0},{10,2},{16,8},{18,10},{24,16},{26,18},{28,24},{30,26},{20,28... | collective-permute-start | bytes 786440 | tf_op jit(solution)/shard_map/ppermute | solution.py:331
  403.1 11.7 %collective-permute-start.71 = (bf16[256,512]{1,0:T(8,128)(2,1)S(1)}, bf16[256,512]{1,0:T(8,128)(2,1)S(1)}, u32[]{:S(2)}, u32[]{:S(2)}) collective-permute-start(bf16[256,512]{1,0:T(8,128)(2,1)S(1)} %fusion.23), channel_id=1, source_target_pairs={{0,8},{2,10},{8,16},{10,18},{16,24},{18,26},{24,28},{26,30},{28,20... | collective-permute-start | bytes 786440 | tf_op jit(solution)/shard_map/ppermute | solution.py:327
  406.9 7.8 %collective-permute-start.78 = (f32[34,512]{1,0:T(8,128)S(1)}, f32[34,512]{1,0:T(8,128)S(1)}, u32[]{:S(2)}, u32[]{:S(2)}) collective-permute-start(f32[34,512]{1,0:T(8,128)S(1)} %fusion.48), channel_id=1, source_target_pairs={{0,4},{2,6},{4,0},{6,2},{8,12},{10,14},{12,8},{14,10},{16,20},{18,... | collective-permute-start | bytes 208904 | tf_op jit(solution)/shard_map/ppermute | solution.py:117
  414.7 4.7 %collective-permute-start.79 = (f32[34,512]{1,0:T(8,128)S(1)}, f32[34,512]{1,0:T(8,128)S(1)}, u32[]{:S(2)}, u32[]{:S(2)}) collective-permute-start(f32[34,512]{1,0:T(8,128)S(1)} %add.415), channel_id=1, source_target_pairs={{0,8},{2,10},{4,12},{6,14},{8,0},{10,2},{12,4},{14,6},{16,24},{18,... | collective-permute-start | bytes 208904 | tf_op jit(solution)/shard_map/ppermute | solution.py:117
  416.2 13.3 %collective-permute-start.72 = (bf16[256,512]{1,0:T(8,128)(2,1)S(1)}, bf16[256,512]{1,0:T(8,128)(2,1)S(1)}, u32[]{:S(2)}, u32[]{:S(2)}) collective-permute-start(bf16[256,512]{1,0:T(8,128)(2,1)S(1)} %get-tuple-element.330), channel_id=1, source_target_pairs={{0,8},{2,10},{8,16},{10,18},{16,24},{18,26},{24,28},{26,30},{28,20... | collective-permute-start | bytes 786440 | tf_op jit(solution)/shard_map/ppermute | solution.py:327
  418.3 11.3 %collective-permute-start.74 = (bf16[256,512]{1,0:T(8,128)(2,1)S(1)}, bf16[256,512]{1,0:T(8,128)(2,1)S(1)}, u32[]{:S(2)}, u32[]{:S(2)}) collective-permute-start(bf16[256,512]{1,0:T(8,128)(2,1)S(1)} %get-tuple-element.331), channel_id=1, source_target_pairs={{8,0},{10,2},{16,8},{18,10},{24,16},{26,18},{28,24},{30,26},{20,28... | collective-permute-start | bytes 786440 | tf_op jit(solution)/shard_map/ppermute | solution.py:331
  419.4 8.5 %collective-permute-start.80 = (f32[34,512]{1,0:T(8,128)S(1)}, f32[34,512]{1,0:T(8,128)S(1)}, u32[]{:S(2)}, u32[]{:S(2)}) collective-permute-start(f32[34,512]{1,0:T(8,128)S(1)} %add.416), channel_id=1, source_target_pairs={{0,16},{2,18},{4,20},{6,22},{8,24},{10,26},{12,28},{14,30},{16,0},... | collective-permute-start | bytes 208904 | tf_op jit(solution)/shard_map/ppermute | solution.py:117
  425.6 16.3 %copy-start.77 = (f32[4]{0:T(128)S(1)}, f32[4]{0:T(128)}, u32[]{:S(2)}) copy-start(f32[4]{0:T(128)} %get-tuple-element.306) | copy-start | bytes 52
  430.7 10.2 %collective-permute-start.20 = (bf16[256,512]{1,0:T(8,128)(2,1)S(1)}, bf16[256,512]{1,0:T(8,128)(2,1)}, u32[]{:S(2)}, u32[]{:S(2)}) collective-permute-start(bf16[256,512]{1,0:T(8,128)(2,1)S(1)} %param.20), channel_id=1, source_target_pairs={{24,0},{26,2},{28,4},{30,6},{25,1},{27,3},{29,5},{31,7}} | collective-permute-start | bytes 786440 | tf_op jit(solution)/shard_map/cond/branch_2_fun/ppermute | solution.py:219
  (68 other events, 404.1 us)
Sparse Core Ops, SparseCore 0:
  28.6 70.0 all-gather.2
  101.5 76.9 all-gather.4
  240.4 113.5 reduce-scatter.1
